TPU v7x, 1024 devices: a whole 8x8x8 slice. The times are simulated.
1024 devices in a mesh: tile: 8 (over x), ens: 64 (over z, y), lev: 2 (over core).
Axes of the slice: x: 8, y: 8, z: 8, core: 2. Of those that a mesh axis runs over, the one named last changes fastest.
Arguments:
- prior_ensemble: bfloat16 [64, 4, 2048, 1024], P('ens', 'lev', 'tile')
- measured_mesh_location: int32 [2, 49152], P('lev', 'tile'), may hold values from 114688 to 524287
- measured_reading: float32 [2, 49152], P('lev', 'tile'), may hold values from -8 to 8
- measured_noise_spread: float32 [2, 49152], P('lev', 'tile'), may hold values from 4 to 16
- ocean_mask: int32 [2048], P('tile'), may hold values from 0 to 1, as said below
- holder_device: int32 [2048], P('tile'), may hold values from 0 to 63, as said below
Outputs:
- analysis: bfloat16 [64, 4, 2048, 1024], P(None, 'lev', ('tile', 'ens'))
Inputs may be any that keep to these rules, and one draw needn't show every extreme that they name: `ocean_mask`: wet is 1 for ocean tiles and 0 for land tiles. `holder_device`: in every strip of 256 tiles, each owner holds exactly 4 tiles, ocean or land, and one owner holds 4 ocean tiles.
All inputs are finite; a program needn't handle non-finite values.
Results may differ from a plain program's by a relative error of at most 0.001.
Values may be sent and summed in bfloat16 or wider, within the bound.
A program may use at most 64 MiB of HBM per device.

v0:
```python
import jax
import jax.numpy as jnp
from jax import lax
from jax.sharding import PartitionSpec as P

TS = 32
TCOLS_DEV = 8
CAP = 4
PATCH_POINT_NUM = 1024
STRIPW = 256


def with_halo(block, sides, width):
    for axis, dim in sides:
        count = lax.axis_size(axis)
        forward = [(i, i + 1) for i in range(count - 1)]
        backward = [(target, source) for source, target in forward]
        low = lax.ppermute(
            lax.slice_in_dim(block, block.shape[dim] - width, None, axis=dim), axis, forward
        )
        high = lax.ppermute(lax.slice_in_dim(block, 0, width, axis=dim), axis, backward)
        block = jnp.concatenate([low, block, high], axis=dim)
    return block


def slot_tables(wet_row, owner_row, owners):
    is_wet = wet_row == 1
    onehot = (
        (owner_row[:, None] == jnp.arange(owners, dtype=jnp.int32)[None, :]) & is_wet[:, None]
    ).astype(jnp.int32)
    before = jnp.cumsum(onehot, axis=0) - onehot
    ranking = jnp.sum(before * onehot, axis=1)
    slot_of = owner_row * CAP + ranking
    chosen = (slot_of[None, :] == jnp.arange(owners * CAP, dtype=jnp.int32)[:, None]) & is_wet[
        None, :
    ]
    return chosen.astype(jnp.float32)


def obs_coords(site_index_list, strip_index, existing_patches):
    tile_local = site_index_list // PATCH_POINT_NUM % existing_patches
    cell_local = site_index_list % PATCH_POINT_NUM
    latitude = tile_local // TCOLS_DEV * TS + cell_local // TS
    longitude = strip_index * STRIPW + tile_local % TCOLS_DEV * TS + cell_local % TS
    return (latitude.astype(jnp.float32), longitude.astype(jnp.float32))


def local(
    prior_ensemble,
    measured_mesh_location,
    measured_reading,
    measured_noise_spread,
    ocean_mask,
    holder_device,
):
    kept_lines, depth_quantity_couples, existing_patches, point_patch_slice = prior_ensemble.shape
    nobs = measured_mesh_location.shape[1]
    owners = lax.axis_size("ens")
    members = kept_lines * owners
    strip = lax.axis_index("tile")
    mine = lax.axis_index("ens")
    site_index_list = measured_mesh_location[0]
    tile_value_block = jnp.take(
        prior_ensemble.reshape(
            kept_lines, depth_quantity_couples * existing_patches * point_patch_slice
        ),
        site_index_list,
        axis=1,
    )
    latitude, longitude = obs_coords(site_index_list, strip, existing_patches)
    meta = jnp.stack(
        [measured_reading[0], 1.0 / measured_noise_spread[0], latitude, longitude], axis=0
    )
    every_member = lax.all_gather(tile_value_block, "ens", axis=0, tiled=True)
    stacked = jnp.concatenate([every_member.astype(jnp.float32), meta], axis=0)
    rimmed = with_halo(stacked, (("tile", 1),), nobs)
    values = rimmed[:members]
    info = rimmed[members:]
    mean_obs = jnp.mean(values, axis=0)
    deviation = values - mean_obs
    innovation = info[0] - mean_obs
    chosen_all = slot_tables(ocean_mask, holder_device, owners)
    chosen_mine = lax.dynamic_slice_in_dim(chosen_all, mine * CAP, CAP, axis=0)
    filled = jnp.sum(chosen_mine, axis=1)
    tiles = jnp.arange(existing_patches, dtype=jnp.int32)
    centre_lat = (tiles // TCOLS_DEV * TS).astype(jnp.float32) + (TS - 1) / 2.0
    centre_lon = (tiles % TCOLS_DEV * TS + strip * STRIPW).astype(jnp.float32) + (TS - 1) / 2.0
    slot_lat = jnp.dot(chosen_mine, centre_lat, precision=lax.Precision.HIGHEST)
    slot_lon = jnp.dot(chosen_mine, centre_lon, precision=lax.Precision.HIGHEST)
    length_sq = (STRIPW / 2.0) ** 2
    dist_sq = (info[2][None, :] - slot_lat[:, None]) ** 2 + (
        info[3][None, :] - slot_lon[:, None]
    ) ** 2
    weights = jnp.exp(-dist_sq / (2.0 * length_sq)) * info[1][None, :]

    def gram_one(weight_row):
        scaled = deviation * weight_row
        return (
            jnp.dot(scaled, deviation.T, precision=lax.Precision.HIGHEST),
            jnp.dot(scaled, innovation, precision=lax.Precision.HIGHEST),
        )

    gram, proj = lax.map(gram_one, weights)
    gram, proj = lax.psum((gram, proj), "lev")
    eye = jnp.eye(members, dtype=jnp.float32)
    factor = jnp.linalg.cholesky((members - 1.0) * eye + gram)
    inv_low = jax.scipy.linalg.solve_triangular(
        factor, jnp.broadcast_to(eye, factor.shape), lower=True
    )
    spread = jnp.sqrt(members - 1.0) * jnp.swapaxes(inv_low, 1, 2)
    half = jax.scipy.linalg.solve_triangular(factor, proj[..., None], lower=True)
    mean_weights = jax.scipy.linalg.solve_triangular(factor, half, lower=True, trans=1)[..., 0]
    transform = spread + mean_weights[:, :, None]
    outgoing = jnp.einsum(
        "pt,mvtc->mpvc",
        chosen_all.astype(jnp.bfloat16),
        prior_ensemble,
        preferred_element_type=jnp.float32,
    ).astype(jnp.bfloat16)
    model_vector = lax.all_to_all(outgoing, "ens", split_axis=1, concat_axis=0, tiled=True).astype(
        jnp.float32
    )
    state_mean = jnp.mean(model_vector, axis=0)
    update = jnp.einsum(
        "qmk,mqvc->kvqc",
        transform,
        model_vector - state_mean[None],
        precision=lax.Precision.HIGHEST,
    )
    result = jnp.transpose(state_mean, (1, 0, 2))[None] + update
    result = result * filled[None, None, :, None]
    return result.astype(jnp.bfloat16)


def solution(mesh):
    in_specs = (
        P("ens", "lev", "tile", None),
        P("lev", "tile"),
        P("lev", "tile"),
        P("lev", "tile"),
        P("tile"),
        P("tile"),
    )
    out_specs = P(None, "lev", ("tile", "ens"), None)
    return jax.shard_map(local, mesh=mesh, in_specs=in_specs, out_specs=out_specs, check_vma=False)
```

profile of v0, /device:TPU:1, one launch (start us, length us, event | category | flops | bytes accessed | tf_op | source)
XLA Modules:
  0.0 313.0 jit_solution(12221107202453370508)
XLA Ops:
  6.5 0.8 compare_select_fusion
  7.3 1.2 fusion.41
  8.5 1.5 copy.61
  10.0 0.0 copy-start
  10.0 38.2 %gather_fusion = bf16[6144]{0:T(1024)(128)(2,1)S(1)} fusion(bf16[524288]{0:T(1024)(128)(2,1)S(1)} %bitcast.117, s32[6144]{0:T(1024)S(1)} %broadcast_clamp_fusion), kind=kCustom, calls=%fused_computation | custom fusion | bytes 49152 | tf_op jit(solution)/shard_map/jit(_take)/gather | solution.py:63
  48.2 0.0 copy-start.1
  48.2 0.0 copy-start.4
  48.2 0.1 fusion.40
  48.3 55.3 %all-gather = bf16[64,1,6144]{2,1,0:T(2,128)(2,1)S(1)} all-gather(bf16[1,1,6144]{2,1,0:T(2,128)(2,1)S(1)} %fusion.40), channel_id=1, replica_groups=mesh['tile'=8,'ens'=64,'lev'=2] {'ens'}, dimensions={0}, use_global_device_ids=true | all-gather | bytes 798720 | tf_op jit(solution)/shard_map/all_gather | solution.py:74
  103.6 0.5 copy.71
  104.2 0.3 add_convert_fusion
  104.4 0.5 concatenate.6
  104.9 4.3 %collective-permute-start = (f32[68,6144]{1,0:T(8,128)S(1)}, f32[68,6144]{1,0:T(8,128)}, u32[]{:S(2)}, u32[]{:S(2)}) collective-permute-start(f32[68,6144]{1,0:T(8,128)S(1)} %concatenate.6), channel_id=1, source_target_pairs={{0,128},{128,256},{256,384},{384,512},{512,640},{640,768},{768,896... | collective-permute-start | bytes 5013512 | tf_op jit(solution)/shard_map/ppermute | solution.py:18
  109.3 1.3 collective-permute-start.1
  110.6 0.6 reduce-window.6
  111.2 0.2 slice_reduce_fusion.1
  111.5 0.1 fusion.31
  111.6 1.7 fusion.15
  113.2 2.0 copy.32
  115.3 6.8 %all-to-all-start = ((bf16[1,256,2,1024]{3,2,0,1:T(2,128)(2,1)}), bf16[1,256,2,1024]{3,2,0,1:T(2,128)(2,1)S(1)}, u32[]{:S(2)}, u32[]{:S(2)}) async-start(bf16[1,256,2,1024]{3,2,0,1:T(2,128)(2,1)} %copy.32), calls=%async_computation | async-start | bytes 2097152 | tf_op jit(solution)/shard_map/all_to_all | solution.py:120
  122.1 0.2 all-reduce.2.cloned.1.call-start
  122.4 0.1 copy.38
  122.5 0.1 copy.37
  122.6 0.1 fusion.60
  122.6 0.1 dynamic-slice_reduce_fusion
  122.8 0.1 convolution_bitcast_fusion.1
  122.9 0.1 convolution_bitcast_fusion.2
  123.1 11.6 %collective-permute-done = f32[68,6144]{1,0:T(8,128)} collective-permute-done((f32[68,6144]{1,0:T(8,128)S(1)}, f32[68,6144]{1,0:T(8,128)}, u32[]{:S(2)}, u32[]{:S(2)}) %collective-permute-start) | collective-permute-done | bytes 1671200 | tf_op jit(solution)/shard_map/ppermute | solution.py:18
  134.6 5.1 %collective-permute-done.1 = f32[68,6144]{1,0:T(8,128)} collective-permute-done((f32[68,6144]{1,0:T(8,128)S(1)}, f32[68,6144]{1,0:T(8,128)}, u32[]{:S(2)}, u32[]{:S(2)}) %collective-permute-start.1) | collective-permute-done | bytes 1671200 | tf_op jit(solution)/shard_map/ppermute | solution.py:21
  139.8 2.4 pad_maximum_fusion
  142.2 0.3 slice_reduce_fusion
  142.5 1.9 pad_maximum_fusion.1
  144.4 2.5 slice_subtract_fusion
  146.9 0.2 exponential_multiply_fusion
  147.1 56.6 %while.12 = (s32[]{:T(128)}, f32[4,64,64]{1,2,0:T(8,128)}, f32[4,64]{1,0:T(4,128)S(1)}, f32[4,18432]{1,0:T(4,128)S(1)}, f32[64,18432]{1,0:T(8,128)}, /*index=5*/f32[18432]{0:T(1024)S(1)}, s32[]{:T(128)}, s32[]{:T(128)}) while((s32[]{:T(128)}, f32[4,64,64]{1,2,0:T(8,128)}, f32[4,64]{1,0:T(4,128)S(1)}, f32[4,18432]{1,0:T(4,128)S(1)}, ...), condition=%wide.region_6.7_spmd, body=%wide.region_5.6_spmd.sunk | while | flops 922484736 | bytes 14558557 | solution.py:103
  147.1 0.1 constant_dynamic-slice_fusion.2
  147.2 5.6 %fusion.80 = f32[1,64]{1,0:T(1,128)S(1)} fusion(f32[18432,1]{0,1:T(1,128)S(1)} %bitcast.124, f32[64,18432]{1,0:T(8,128)} %get-tuple-element.123, f32[18432]{0:T(1024)S(1)} %bitcast.118), kind=kOutput, calls=%fused_computation.1.clone.1 | convolution fusion | flops 15335424 | bytes 4866304 | tf_op jit(solution)/shard_map/while/body/eval_jaxpr/dot_general | solution.py:100
  152.8 8.5 %fusion.79 = f32[4,64,64]{1,2,0:T(8,128)} fusion(f32[4,64,64]{1,2,0:T(8,128)} %get-tuple-element.112, s32[]{:T(128)} %get-tuple-element.111, f32[64,18432]{1,0:T(8,128)} %get-tuple-element.123, f32[18432]{0:T(1024)S(1)} %bitcast.119), kind=kOutput, calls=%fused_computation.8.clone.1 | convolution fusion | flops 907149312 | bytes 9544192 | tf_op jit(solution)/shard_map/while/body/eval_jaxpr/dot_general | solution.py:99
  161.3 0.1 constant_dynamic-slice_fusion.2
  161.3 5.6 %fusion.80 = f32[1,64]{1,0:T(1,128)S(1)} fusion(f32[18432,1]{0,1:T(1,128)S(1)} %bitcast.124, f32[64,18432]{1,0:T(8,128)} %get-tuple-element.123, f32[18432]{0:T(1024)S(1)} %bitcast.118), kind=kOutput, calls=%fused_computation.1.clone.1 | convolution fusion | flops 15335424 | bytes 4866304 | tf_op jit(solution)/shard_map/while/body/eval_jaxpr/dot_general | solution.py:100
  166.9 8.5 %fusion.79 = f32[4,64,64]{1,2,0:T(8,128)} fusion(f32[4,64,64]{1,2,0:T(8,128)} %get-tuple-element.112, s32[]{:T(128)} %get-tuple-element.111, f32[64,18432]{1,0:T(8,128)} %get-tuple-element.123, f32[18432]{0:T(1024)S(1)} %bitcast.119), kind=kOutput, calls=%fused_computation.8.clone.1 | convolution fusion | flops 907149312 | bytes 9544192 | tf_op jit(solution)/shard_map/while/body/eval_jaxpr/dot_general | solution.py:99
  175.4 0.1 constant_dynamic-slice_fusion.2
  175.5 5.6 %fusion.80 = f32[1,64]{1,0:T(1,128)S(1)} fusion(f32[18432,1]{0,1:T(1,128)S(1)} %bitcast.124, f32[64,18432]{1,0:T(8,128)} %get-tuple-element.123, f32[18432]{0:T(1024)S(1)} %bitcast.118), kind=kOutput, calls=%fused_computation.1.clone.1 | convolution fusion | flops 15335424 | bytes 4866304 | tf_op jit(solution)/shard_map/while/body/eval_jaxpr/dot_general | solution.py:100
  181.1 8.5 %fusion.79 = f32[4,64,64]{1,2,0:T(8,128)} fusion(f32[4,64,64]{1,2,0:T(8,128)} %get-tuple-element.112, s32[]{:T(128)} %get-tuple-element.111, f32[64,18432]{1,0:T(8,128)} %get-tuple-element.123, f32[18432]{0:T(1024)S(1)} %bitcast.119), kind=kOutput, calls=%fused_computation.8.clone.1 | convolution fusion | flops 907149312 | bytes 9544192 | tf_op jit(solution)/shard_map/while/body/eval_jaxpr/dot_general | solution.py:99
  189.5 0.1 constant_dynamic-slice_fusion.2
  189.6 5.6 %fusion.80 = f32[1,64]{1,0:T(1,128)S(1)} fusion(f32[18432,1]{0,1:T(1,128)S(1)} %bitcast.124, f32[64,18432]{1,0:T(8,128)} %get-tuple-element.123, f32[18432]{0:T(1024)S(1)} %bitcast.118), kind=kOutput, calls=%fused_computation.1.clone.1 | convolution fusion | flops 15335424 | bytes 4866304 | tf_op jit(solution)/shard_map/while/body/eval_jaxpr/dot_general | solution.py:100
  195.2 8.5 %fusion.79 = f32[4,64,64]{1,2,0:T(8,128)} fusion(f32[4,64,64]{1,2,0:T(8,128)} %get-tuple-element.112, s32[]{:T(128)} %get-tuple-element.111, f32[64,18432]{1,0:T(8,128)} %get-tuple-element.123, f32[18432]{0:T(1024)S(1)} %bitcast.119), kind=kOutput, calls=%fused_computation.8.clone.1 | convolution fusion | flops 907149312 | bytes 9544192 | tf_op jit(solution)/shard_map/while/body/eval_jaxpr/dot_general | solution.py:99
  203.7 0.0 all-reduce.2.cloned.1.call-update
  203.7 14.9 %psum.15 = f32[4,64]{1,0:T(4,128)S(1)} all-reduce(f32[4,64]{1,0:T(4,128)S(1)} %get-tuple-element.39), channel_id=1, replica_groups=mesh['tile'=8,'ens'=64,'lev'=2] {'lev'}, use_global_device_ids=true, to_apply=%region_10.11 | all-reduce | flops 256 | bytes 2048 | tf_op jit(solution)/shard_map/psum | solution.py:104
  218.6 34.3 %all-reduce.2.cloned.1.call-done = f32[4,64,64]{1,2,0:T(8,128)} async-done(((f32[4,64,64]{1,2,0:T(8,128)}), f32[4,64,64]{1,2,0:T(8,128)}) %all-reduce.2.cloned.1.call-update) | async-done | bytes 65552 | tf_op jit(solution)/shard_map/psum | solution.py:104
  252.9 0.9 broadcast_add_fusion
  253.9 0.1 copy.40
  254.0 0.9 fusion.25
  254.9 23.5 %custom-call.14 = f32[4,64,64]{2,1,0:T(8,128)S(1)} custom-call(f32[4,64,64]{2,1,0:T(8,128)S(1)} %fusion.25), custom_call_target="Cholesky" | custom-call | tf_op jit(solution)/shard_map/jit(cholesky)/cholesky | solution.py:106
  278.4 0.1 compare_reduce_fusion
  278.5 0.1 select_bitcast_fusion
  278.6 19.7 %custom-call.15 = f32[4,1,64,64]{2,3,1,0:T(8,128)S(1)} custom-call(f32[4,1,64,64]{3,2,1,0:T(8,128)S(1)} %select_bitcast_fusion), custom_call_target="InvertDiagBlocksLowerTriangular" | custom-call | tf_op jit(solution)/shard_map/jit(_solve_triangular)/vmap()/triangular_solve | solution.py:107
  298.3 0.2 convolution_bitcast_fusion
  298.5 0.3 fusion.21
  298.8 0.3 fusion.17
  299.1 0.9 convert_reduce_fusion
  299.9 0.9 convert.1
  300.9 3.4 %fusion.13 = bf16[64,2,4,1024]{3,0,1,2:T(8,128)(2,1)S(1)} fusion(f32[4,64,64,1]{2,1,3,0:T(8,128)S(1)} %fusion.17, f32[64,4,2,1024]{3,2,1,0:T(2,128)S(1)} %convert.1, f32[4]{0:T(128)S(1)} %dynamic-slice_reduce_fusion, f32[4,2,1024]{2,1,0:T(2,128)S(1)} %copy.35, f32[2,4,1024]{2,0,1:T(2,128)S(1)} %copy.34), kind=kOutput, calls=%fused_computation.15 | convolution fusion | flops 404750336 | bytes 3276816 | tf_op jit(solution)/shard_map/qmk,mqvc->kvqc/dot_general | solution.py:124
  304.3 1.8 copy.43
  (33 shorter events, 0.5 us)
Async XLA Ops:
  10.0 38.2 %copy-start = (s32[1,6144]{1,0:T(1,128)S(1)}, s32[1,6144]{1,0:T(1,128)}, u32[]{:S(2)}) copy-start(s32[1,6144]{1,0:T(1,128)} %param.9) | copy-start | bytes 73732
  48.2 55.9 %copy-start.2 = (f32[1,6144]{1,0:T(1,128)S(1)}, f32[1,6144]{1,0:T(1,128)}, u32[]{:S(2)}) copy-start(f32[1,6144]{1,0:T(1,128)} %param.11) | copy-start | bytes 73732
  48.2 56.2 %copy-start.1 = (f32[1,6144]{1,0:T(1,128)S(1)}, f32[1,6144]{1,0:T(1,128)}, u32[]{:S(2)}) copy-start(f32[1,6144]{1,0:T(1,128)} %param.10) | copy-start | bytes 73732
  48.2 62.4 %copy-start.4 = (s32[256]{0:T(256)S(1)}, s32[256]{0:T(256)}, u32[]{:S(2)}) copy-start(s32[256]{0:T(256)} %param.12) | copy-start | bytes 3076
  48.2 62.4 %copy-start.3 = (s32[256]{0:T(256)S(1)}, s32[256]{0:T(256)}, u32[]{:S(2)}) copy-start(s32[256]{0:T(256)} %param.13) | copy-start | bytes 3076
  104.9 29.7 %collective-permute-start = (f32[68,6144]{1,0:T(8,128)S(1)}, f32[68,6144]{1,0:T(8,128)}, u32[]{:S(2)}, u32[]{:S(2)}) collective-permute-start(f32[68,6144]{1,0:T(8,128)S(1)} %concatenate.6), channel_id=1, source_target_pairs={{0,128},{128,256},{256,384},{384,512},{512,640},{640,768},{768,896... | collective-permute-start | bytes 5013512 | tf_op jit(solution)/shard_map/ppermute | solution.py:18
  109.3 30.5 %collective-permute-start.1 = (f32[68,6144]{1,0:T(8,128)S(1)}, f32[68,6144]{1,0:T(8,128)}, u32[]{:S(2)}, u32[]{:S(2)}) collective-permute-start(f32[68,6144]{1,0:T(8,128)S(1)} %concatenate.6), channel_id=1, source_target_pairs={{128,0},{256,128},{384,256},{512,384},{640,512},{768,640},{896,768... | collective-permute-start | bytes 5013512 | tf_op jit(solution)/shard_map/ppermute | solution.py:21
  115.3 183.8 %all-to-all-start = ((bf16[1,256,2,1024]{3,2,0,1:T(2,128)(2,1)}), bf16[1,256,2,1024]{3,2,0,1:T(2,128)(2,1)S(1)}, u32[]{:S(2)}, u32[]{:S(2)}) async-start(bf16[1,256,2,1024]{3,2,0,1:T(2,128)(2,1)} %copy.32), calls=%async_computation | async-start | bytes 2097152 | tf_op jit(solution)/shard_map/all_to_all | solution.py:120
  122.1 130.8 %all-reduce.2.cloned.1.call-start = ((), (), s32[]{:S(2)}) async-start(), calls=%async_computation.1 | async-start | bytes 262144 | tf_op jit(solution)/shard_map/psum | solution.py:104
Sparse Core Ops, SparseCore 0:
  203.8 49.0 all-reduce.1
where the time goes:
time: 314 us; the launch traced here: 313 us
  blocking collectives  70.2 us (22%)
  matrix products  62.3 us (20%)
  other arithmetic  57.6 us (18%)
  waiting for transfers between devices  51 us (16%)
  local copies, waits for them, and re-layouts  45.4 us (14%)
  between operations  13.8 us (4%)
  starting transfers between devices  12.7 us (4%)
    all_gather x1, blocking collectives, local(): every_member = lax.all_gather(tile_value_block, 'ens', axis=0, tiled=True)  55.3 us
    gather x1, local copies, waits for them, and re-layouts, local(): jnp.take(prior_ensemble.reshape(kept_lines, depth_quantity_couples * exis...  38.2 us
    psum x1, waiting for transfers between devices, local(): gram, proj = lax.psum((gram, proj), 'lev')  34.3 us
    dot_general x4, matrix products, gram_one(): jnp.dot(scaled, deviation.T, precision=lax.Precision.HIGHEST)  33.9 us
    another operation x3, other arithmetic, local(): factor = jnp.linalg.cholesky((members - 1.0) * eye + gram)  23.6 us
    dot_general x4, matrix products, gram_one(): jnp.dot(scaled, innovation, precision=lax.Precision.HIGHEST)  22.3 us
    another operation x3, other arithmetic, local(): jax.scipy.linalg.solve_triangular(factor, jnp.broadcast_to(eye, factor.sh...  19.8 us
    psum x1, blocking collectives, local(): gram, proj = lax.psum((gram, proj), 'lev')  14.9 us
  transfers between devices with their start and end apart: 4, of which 3 were waited for; matrix products, arithmetic and copies ran while one was open for 37% of the time, Pallas kernels for 0%

commit v1 on v0

v1 whole, which is shorter than its diff:
```python
import functools
import jax
import jax.numpy as jnp
from jax import lax
from jax.experimental import pallas as pl
from jax.experimental.pallas import tpu as pltpu
from jax.sharding import PartitionSpec as P

TS = 32
CAP = 4
OWNERS = 64
MEMBERS = 64
STRIPS = 8
TILES = 256
CELLS = 1024
STRIPW = 256
ROWS = 48
FIRST_ROW = 112
LENGTH_SQ = (STRIPW / 2.0) ** 2
BLK = 72
MESH = pl.DeviceIdType.MESH
VLIM = 48 * 1024 * 1024


def prep_kernel(prior, idx, mask, holder, vals, outg, coords, fvals):
    strip = lax.axis_index("tile")
    mine = lax.axis_index("ens")
    owner = holder[...]
    wet = mask[...] == 1
    key = jnp.where(wet, owner, -1).astype(jnp.float32)
    key_all = jnp.broadcast_to(key, (TILES, TILES))
    key_t = key_all.T
    earlier = lax.broadcasted_iota(jnp.int32, (TILES, TILES), 0) < lax.broadcasted_iota(
        jnp.int32, (TILES, TILES), 1
    )
    same = (key_all == key_t) & earlier
    rank = jnp.sum(jnp.where(same, 1.0, 0.0), axis=0, keepdims=True).astype(jnp.int32)
    slot = jnp.where(wet, owner * CAP + rank, -1)
    tile = lax.broadcasted_iota(jnp.int32, (1, TILES), 1)
    half = (TS - 1) / 2.0
    clat = (tile // 8 * TS).astype(jnp.float32) + half
    clon = (tile % 8 * TS + strip * STRIPW).astype(jnp.float32) + half
    lats, lons, fills = [], [], []
    for q in range(CAP):
        here = slot == mine * CAP + q
        for into, what in ((lats, clat), (lons, clon), (fills, jnp.ones_like(clat))):
            total = jnp.sum(jnp.where(here, what, 0.0), axis=1, keepdims=True)
            into.append(jnp.broadcast_to(total, (1, 128)))
    coords[...] = jnp.concatenate(lats + lons + fills + fills, axis=0)
    rows = lax.broadcasted_iota(jnp.int32, (OWNERS * 16, 2 * TILES), 0)
    total = None
    for h in range(2):
        target = jnp.concatenate([slot * 4 + h, slot * 4 + 2 + h], axis=1)
        target = jnp.where(jnp.concatenate([wet, wet], axis=1), target, -1)
        pick = jnp.where(rows == target, 1.0, 0.0).astype(jnp.bfloat16)
        part = jnp.dot(
            pick, prior[:, h * 512 : (h + 1) * 512], preferred_element_type=jnp.float32
        )
        total = part if total is None else total + part
    outg[...] = total.astype(jnp.bfloat16).reshape(OWNERS, 16, 512)

    def step(j, carry):
        ids = idx[pl.ds(j * 4, 4), :]
        pieces, highs = [], []
        cell = lax.broadcasted_iota(jnp.int32, (CELLS, 128), 0)
        for i in range(4):
            row = ids[i : i + 1, :]
            pieces.append(jnp.where(cell == (row & (CELLS - 1)), 1.0, 0.0).astype(jnp.bfloat16))
            highs.append((row >> 10) - FIRST_ROW)
        onehot = jnp.concatenate(pieces, axis=1)
        high = jnp.concatenate(highs, axis=1)
        got = jnp.dot(prior[FIRST_ROW:, :], onehot, preferred_element_type=jnp.float32)
        line = lax.broadcasted_iota(jnp.int32, got.shape, 0)
        value = jnp.sum(jnp.where(line == high, got, 0.0), axis=0, keepdims=True)
        for i in range(4):
            fvals[pl.ds(j * 4 + i, 1), :] = value[:, i * 128 : (i + 1) * 128]
        return carry

    lax.fori_loop(0, ROWS // 4, step, 0)
    vals[...] = fvals[...].astype(jnp.bfloat16)


def prep(prior, idx, mask, holder):
    return pl.pallas_call(
        prep_kernel,
        out_shape=(
            jax.ShapeDtypeStruct((ROWS, 128), jnp.bfloat16),
            jax.ShapeDtypeStruct((OWNERS, 16, 512), jnp.bfloat16),
            jax.ShapeDtypeStruct((16, 128), jnp.float32),
        ),
        in_specs=[pl.BlockSpec(memory_space=pltpu.VMEM)] * 4,
        out_specs=[pl.BlockSpec(memory_space=pltpu.VMEM)] * 3,
        scratch_shapes=[pltpu.VMEM((ROWS, 128), jnp.float32)],
        compiler_params=pltpu.CompilerParams(vmem_limit_bytes=VLIM),
        name="prep",
    )(prior, idx, mask, holder)


def weights_into(wscr, idx, noise, tlat, tlon, strip):
    def step(r, carry):
        ids = idx[pl.ds(r, 1), :]
        tile = (ids >> 10) & (TILES - 1)
        cell = ids & (CELLS - 1)
        lat = ((tile >> 3) * TS + (cell >> 5)).astype(jnp.float32)
        lon = (strip * STRIPW + (tile & 7) * TS + (cell & (TS - 1))).astype(jnp.float32)
        dist = (lat - tlat) ** 2 + (lon - tlon) ** 2
        wscr[r] = jnp.exp(-dist / (2.0 * LENGTH_SQ)) * (1.0 / noise[pl.ds(r, 1), :])
        return carry

    lax.fori_loop(0, ROWS, step, 0)


def split(x):
    high = x.astype(jnp.bfloat16)
    low = (x - high.astype(jnp.float32)).astype(jnp.bfloat16)
    return high, low


def gram_steps(fbuf, rows, first, wscr, read, acc):
    def step(k, carry):
        r0 = 2 * k
        x = jnp.concatenate(
            [fbuf[pl.ds(r0 + i, MEMBERS, stride=rows), :] for i in range(2)], axis=1
        )
        mean = jnp.sum(x, axis=0, keepdims=True) * (1.0 / MEMBERS)
        dev = x - mean
        reading = jnp.concatenate([read[pl.ds(first + r0 + i, 1), :] for i in range(2)], axis=1)
        inno = reading - mean
        w = jnp.concatenate([wscr[first + r0], wscr[first + r0 + 1]], axis=1)
        high, low = split(dev)
        right = jnp.concatenate([high, low], axis=0)
        winno = w * inno
        top = lax.broadcasted_iota(jnp.int32, (8, 256), 0) == 0
        blocks = []
        for t in range(12):
            blocks.append(dev * w[t : t + 1, :])
            blocks.append(jnp.where(top, winno[t : t + 1, :], 0.0))
        left = jnp.concatenate(blocks, axis=0)
        lh, ll = split(left)
        dims = (((1,), (1,)), ((), ()))
        acc[...] += lax.dot_general(
            lh, right, dims, preferred_element_type=jnp.float32
        ) + lax.dot_general(ll, right, dims, preferred_element_type=jnp.float32)
        return carry

    lax.fori_loop(0, rows // 2, step, 0)


def main_kernel(
    vals, idx, read, noise, coords, outg, gsum, recv,
    buf_a, buf_b, fa, fb, wscr, cbuf, acc, gp, gr, tot, lr,
    s_own, s_a1, r_a1, s_b1, r_b1, s_a2, r_a2, s_b2, r_b2,
    s_x, r_x, s_c, r_c, s_g, r_g, s_l, r_l,
):
    strip = lax.axis_index("tile")
    ens = lax.axis_index("ens")
    lev = lax.axis_index("lev")
    y, z = ens % 8, ens // 8
    i1, i2 = y + lev * (z - y), z + lev * (y - z)
    n1, n2 = 1 + 7 * lev, 8 - 7 * lev
    low, high = (strip + STRIPS - 1) % STRIPS, (strip + 1) % STRIPS

    barrier = pltpu.get_barrier_semaphore()

    def greet(d, carry):
        pl.semaphore_signal(
            barrier, inc=1, device_id={"ens": (ens + d) % OWNERS}, device_id_type=MESH
        )
        return carry

    lax.fori_loop(1, OWNERS, greet, 0)
    for where in ({"tile": low}, {"tile": high}, {"lev": 1 - lev}):
        pl.semaphore_signal(barrier, inc=1, device_id=where, device_id_type=MESH)
    pl.semaphore_wait(barrier, OWNERS - 1 + 3)

    def send(src, dst, ss, rs, where):
        pltpu.make_async_remote_copy(
            src_ref=src, dst_ref=dst, send_sem=ss, recv_sem=rs, device_id=where,
            device_id_type=MESH,
        ).start()

    def wait_for(ref, sem):
        pltpu.make_async_copy(ref, ref, sem).wait()

    own_a = pltpu.make_async_copy(vals.at[pl.ds(0, 32)], buf_a.at[i2, i1], s_own.at[0])
    own_b = pltpu.make_async_copy(vals.at[pl.ds(32, 16)], buf_b.at[i1, i2], s_own.at[1])
    own_x = pltpu.make_async_copy(outg.at[ens], recv.at[ens], s_own.at[2])
    own_a.start()
    own_b.start()

    send(coords, cbuf.at[1], s_c.at[0], r_c.at[1], {"tile": low})
    send(coords, cbuf.at[0], s_c.at[1], r_c.at[0], {"tile": high})

    def first_a(d, carry):
        p = (i1 + d) % 8
        send(vals.at[pl.ds(0, 32)], buf_a.at[i2, i1], s_a1, r_a1, {"ens": p * n1 + i2 * n2})
        return carry

    def first_b(d, carry):
        p = (i2 + d) % 8
        send(vals.at[pl.ds(32, 16)], buf_b.at[i1, i2], s_b1, r_b1, {"ens": i1 * n1 + p * n2})
        return carry

    def second_a(d, carry):
        p = (i2 + d) % 8
        send(buf_a.at[i2], buf_a.at[i2], s_a2, r_a2, {"ens": i1 * n1 + p * n2})
        return carry

    def second_b(d, carry):
        p = (i1 + d) % 8
        send(buf_b.at[i1], buf_b.at[i1], s_b2, r_b2, {"ens": p * n1 + i2 * n2})
        return carry

    lax.fori_loop(1, 8, first_a, 0)
    lax.fori_loop(1, 8, first_b, 0)
    own_a.wait()
    wait_for(buf_a.at[0, pl.ds(0, 7)], r_a1)
    lax.fori_loop(1, 8, second_a, 0)
    own_b.wait()
    wait_for(buf_b.at[0, pl.ds(0, 7)], r_b1)
    lax.fori_loop(1, 8, second_b, 0)

    own_x.start()

    def exchange(d, carry):
        other = (ens + d) % OWNERS
        send(outg.at[other], recv.at[ens], s_x, r_x, {"ens": other})
        return carry

    lax.fori_loop(1, OWNERS, exchange, 0)

    wait_for(cbuf.at[0], r_c.at[0])
    wait_for(cbuf.at[1], r_c.at[1])
    pad = jnp.zeros((4, 128), jnp.float32)
    tlat = jnp.concatenate([cbuf[0, 0:4], coords[0:4], cbuf[1, 0:4], pad], axis=0)
    tlon = jnp.concatenate([cbuf[0, 4:8], coords[4:8], cbuf[1, 4:8], pad], axis=0)
    weights_into(wscr, idx, noise, tlat, tlon, strip)
    acc[...] = jnp.zeros_like(acc)

    wait_for(buf_b.at[pl.ds(0, 7)], r_b2)

    def widen_b(k, carry):
        a, b = k // 8, k % 8
        m = a * n1 + b * n2
        fb[pl.ds(pl.multiple_of(m * 16, 16), 16), :] = buf_b[a, b].astype(jnp.float32)
        return carry

    lax.fori_loop(0, MEMBERS, widen_b, 0)
    gram_steps(fb, 16, 32, wscr, read, acc)

    wait_for(buf_a.at[pl.ds(0, 7)], r_a2)

    def widen_a(k, carry):
        a, b = k // 8, k % 8
        m = b * n1 + a * n2
        fa[pl.ds(pl.multiple_of(m * 32, 32), 32), :] = buf_a[a, b].astype(jnp.float32)
        return carry

    lax.fori_loop(0, MEMBERS, widen_a, 0)
    gram_steps(fa, 32, 0, wscr, read, acc)

    for g in range(3):
        for p in range(2):
            sides = []
            for q in range(2):
                t = g * 4 + p * 2 + q
                block = acc[t * BLK : (t + 1) * BLK, :]
                sides.append(block[:, :64] + block[:, 64:])
            gp[g, p] = jnp.concatenate(sides, axis=1)
    send(gp.at[0], gr.at[1], s_g.at[0], r_g.at[1], {"tile": low})
    send(gp.at[2], gr.at[0], s_g.at[1], r_g.at[0], {"tile": high})
    wait_for(gr.at[0], r_g.at[0])
    wait_for(gr.at[1], r_g.at[1])
    tot[...] = (
        gp[1]
        + jnp.where(strip > 0, gr[0], jnp.zeros_like(gr[0]))
        + jnp.where(strip < STRIPS - 1, gr[1], jnp.zeros_like(gr[1]))
    )
    send(tot, lr, s_l, r_l, {"lev": 1 - lev})
    wait_for(lr, r_l)
    gsum[...] = tot[...] + lr[...]

    own_x.wait()
    wait_for(recv.at[pl.ds(0, OWNERS - 1)], r_x)
    wait_for(outg.at[pl.ds(0, OWNERS - 1)], s_x)
    wait_for(buf_a.at[0, pl.ds(0, 7)], s_a1)
    wait_for(buf_b.at[0, pl.ds(0, 7)], s_b1)
    wait_for(buf_a.at[pl.ds(0, 7)], s_a2)
    wait_for(buf_b.at[pl.ds(0, 7)], s_b2)
    for i in range(2):
        wait_for(coords, s_c.at[i])
        wait_for(gp.at[0], s_g.at[i])
    wait_for(tot, s_l)


def spread_out(vals, idx, read, noise, coords, outg):
    dma = pltpu.SemaphoreType.DMA
    vmem = pl.BlockSpec(memory_space=pltpu.VMEM)
    any_ = pl.BlockSpec(memory_space=pl.ANY)
    return pl.pallas_call(
        main_kernel,
        out_shape=(
            jax.ShapeDtypeStruct((2, BLK, 128), jnp.float32),
            jax.ShapeDtypeStruct((MEMBERS, 16, 512), jnp.bfloat16),
        ),
        in_specs=[vmem] * 5 + [any_],
        out_specs=[vmem, any_],
        scratch_shapes=[
            pltpu.VMEM((8, 8, 32, 128), jnp.bfloat16),
            pltpu.VMEM((8, 8, 16, 128), jnp.bfloat16),
            pltpu.VMEM((MEMBERS * 32, 128), jnp.float32),
            pltpu.VMEM((MEMBERS * 16, 128), jnp.float32),
            pltpu.VMEM((ROWS, 16, 128), jnp.float32),
            pltpu.VMEM((2, 16, 128), jnp.float32),
            pltpu.VMEM((12 * BLK, 128), jnp.float32),
            pltpu.VMEM((3, 2, BLK, 128), jnp.float32),
            pltpu.VMEM((2, 2, BLK, 128), jnp.float32),
            pltpu.VMEM((2, BLK, 128), jnp.float32),
            pltpu.VMEM((2, BLK, 128), jnp.float32),
            dma((3,)),
            dma, dma, dma, dma, dma, dma, dma, dma,
            dma, dma,
            dma((2,)), dma((2,)), dma((2,)), dma((2,)),
            dma, dma,
        ],
        compiler_params=pltpu.CompilerParams(
            collective_id=1, has_side_effects=True, vmem_limit_bytes=VLIM
        ),
        name="spread",
    )(vals, idx, read, noise, coords, outg)


def finish_kernel(gsum, coords, recv, out, wide, res):
    for c in range(4):
        wide[c] = recv[:, :, c * 128 : (c + 1) * 128].astype(jnp.float32).reshape(-1, 128)
    row = lax.broadcasted_iota(jnp.int32, (MEMBERS, 128), 0)
    lane = lax.broadcasted_iota(jnp.int32, (MEMBERS, 128), 1)
    eye = row == lane
    eye_r = row + MEMBERS == lane
    mats, projs = [], []
    for q in range(CAP):
        pair = gsum[q // 2]
        if q % 2:
            pair = jnp.concatenate([pair[:, 64:], pair[:, :64]], axis=1)
        body = pair[:64] + jnp.where(eye, MEMBERS - 1.0, 0.0)
        mats.append(jnp.where(lane < 64, body, jnp.where(eye_r, 1.0, 0.0)))
        projs.append(pair[64:65])
    mats = [[m[8 * v : 8 * v + 8] for v in range(8)] for m in mats]
    sub = lax.broadcasted_iota(jnp.int32, (8, 128), 0)
    for j in range(MEMBERS):
        v0, r = j // 8, j % 8
        for q in range(CAP):
            m = mats[q]
            prow = m[v0][r : r + 1, :]
            piv = prow[:, j : j + 1]
            scaled = prow / piv
            for v in range(v0, 8):
                col = m[v][:, j : j + 1]
                if v == v0:
                    if r == 7:
                        continue
                    col = jnp.where(sub[:, :1] > r, col, 0.0)
                m[v] = m[v] - col * scaled
    for q in range(CAP):
        m = jnp.concatenate(mats[q], axis=0)
        diag = jnp.sum(jnp.where(eye, m, 0.0), axis=1, keepdims=True)
        inv = m[:, 64:] * lax.rsqrt(diag)
        proj = projs[q][:, :64]
        zed = jnp.sum(inv * proj, axis=1, keepdims=True)
        mean_w = jnp.sum(inv * zed, axis=0, keepdims=True)
        trans = inv * (MEMBERS - 1.0) ** 0.5 + mean_w
        trans = trans + (1.0 - jnp.sum(trans, axis=1, keepdims=True)) * (1.0 / MEMBERS)
        trans = trans * coords[8 + q : 9 + q, :64]
        t0 = trans.astype(jnp.bfloat16)
        rest = trans - t0.astype(jnp.float32)
        t1, t2 = split(rest)
        left = jnp.concatenate([t0, t1, t2], axis=0)
        for v in range(2):
            for h in range(2):
                r = q * 4 + v * 2 + h
                x = jnp.concatenate(
                    [wide[c, pl.ds(r, MEMBERS, stride=16), :] for c in range(4)], axis=1
                ).astype(jnp.bfloat16)
                got = jnp.dot(left, x, preferred_element_type=jnp.float32)
                got = got[:64] + (got[64:128] + got[128:])
                for c in range(4):
                    res[h * 4 + c, pl.ds(v * 4 + q, MEMBERS, stride=8), :] = got[
                        :, c * 128 : (c + 1) * 128
                    ]
    for c in range(8):
        body = res[c].reshape(MEMBERS, 2, CAP, 128).astype(jnp.bfloat16)
        out[:, :, :, c * 128 : (c + 1) * 128] = body


def finish(gsum, coords, recv):
    return pl.pallas_call(
        finish_kernel,
        out_shape=jax.ShapeDtypeStruct((MEMBERS, 2, CAP, CELLS), jnp.bfloat16),
        in_specs=[pl.BlockSpec(memory_space=pltpu.VMEM)] * 3,
        out_specs=pl.BlockSpec(memory_space=pltpu.VMEM),
        scratch_shapes=[
            pltpu.VMEM((4, MEMBERS * 16, 128), jnp.float32),
            pltpu.VMEM((8, MEMBERS * 8, 128), jnp.float32),
        ],
        compiler_params=pltpu.CompilerParams(vmem_limit_bytes=VLIM),
        name="finish",
    )(gsum, coords, recv)


def local(prior, location, reading, noise, ocean, holder):
    prior = prior.reshape(2 * TILES, CELLS)
    idx = location.reshape(ROWS, 128)
    read = reading.reshape(ROWS, 128)
    spread = noise.reshape(ROWS, 128)
    vals, outg, coords = prep(prior, idx, ocean.reshape(1, TILES), holder.reshape(1, TILES))
    gsum, recv = spread_out(vals, idx, read, spread, coords, outg)
    return finish(gsum, coords, recv)


def solution(mesh):
    in_specs = (
        P("ens", "lev", "tile", None),
        P("lev", "tile"),
        P("lev", "tile"),
        P("lev", "tile"),
        P("tile"),
        P("tile"),
    )
    out_specs = P(None, "lev", ("tile", "ens"), None)
    return jax.shard_map(local, mesh=mesh, in_specs=in_specs, out_specs=out_specs, check_vma=False)
```

time: 314 us -> 108 us (0.34)
  Pallas kernels: 0 us -> 105 us
  blocking collectives: 70.2 us -> 0 us
  matrix products: 62.3 us -> 0 us
  other arithmetic: 57.6 us -> 0 us
  waiting for transfers between devices: 51 us -> 0 us
  local copies, waits for them, and re-layouts: 45.4 us -> 2.66 us
  between operations: 13.8 us -> 0.03 us
  starting transfers between devices: 12.7 us -> 0 us
    pallas_call x0 -> x3, Pallas kernels: none -> 105 us  [the longest x1 86.9 us: spread_out(): pl.pallas_call(main_kernel, out_shape=(jax.ShapeDtypeStruct((2, BLK, 128)...]
    dot_general x12 -> x0, matrix products: 61.5 us -> none  [the longest x4 33.9 us: gram_one(): jnp.dot(scaled, deviation.T, precision=lax.Precision.HIGHEST)]
    all_gather x1 -> x0, blocking collectives: 55.3 us -> none  [local(): every_member = lax.all_gather(tile_value_block, 'ens', axis=0, tiled=True)]
    another operation x8 -> x0, other arithmetic: 44 us -> none  [the longest x3 23.6 us: local(): factor = jnp.linalg.cholesky((members - 1.0) * eye + gram)]
    gather x1 -> x0, local copies, waits for them, and re-layouts: 38.2 us -> none  [local(): jnp.take(prior_ensemble.reshape(kept_lines, depth_quantity_couples * exis...]
    psum x1 -> x0, waiting for transfers between devices: 34.3 us -> none  [local(): gram, proj = lax.psum((gram, proj), 'lev')]
    ppermute x2 -> x0, waiting for transfers between devices: 16.7 us -> none  [the longest x1 11.6 us: with_halo(): lax.ppermute(lax.slice_in_dim(block, block.shape[dim] - width, None, axis...]
    psum x1 -> x0, blocking collectives: 14.9 us -> none  [local(): gram, proj = lax.psum((gram, proj), 'lev')]
  transfers between devices with their start and end apart: 4 -> 0, of which waited for: 3 -> 0; matrix products, arithmetic and copies ran while one was open for 37% -> 0% of each run, Pallas kernels for 0% -> 0%
where the time goes in v1:
time: 108 us
  Pallas kernels  105 us (97%)
  local copies, waits for them, and re-layouts  2.66 us (2%)
    pallas_call x1, Pallas kernels, spread_out(): pl.pallas_call(main_kernel, out_shape=(jax.ShapeDtypeStruct((2, BLK, 128)...  86.9 us
    pallas_call x1, Pallas kernels, finish(): pl.pallas_call(finish_kernel, out_shape=jax.ShapeDtypeStruct((MEMBERS, 2,...  9.45 us
    pallas_call x1, Pallas kernels, prep(): pl.pallas_call(prep_kernel, out_shape=(jax.ShapeDtypeStruct((ROWS, 128),...  8.65 us
    unnamed x12, local copies, waits for them, and re-layouts  2.66 us

profile of v1, /device:TPU:1, one launch (start us, length us, event | category | flops | bytes accessed | tf_op | source)
XLA Modules:
  0.0 107.7 jit_solution(12927201524956285919)
XLA Ops:
  0.0 0.0 copy-start.5
  0.0 0.0 copy-start.4
  0.0 0.7 copy-done.5
  0.7 0.0 copy-done.4
  0.7 0.0 copy-start
  0.7 1.2 %copy-done = bf16[1,2,256,1024]{3,2,1,0:T(8,128)(2,1)S(1)} copy-done((bf16[1,2,256,1024]{3,2,1,0:T(8,128)(2,1)S(1)}, bf16[1,2,256,1024]{3,2,1,0:T(8,128)(2,1)}, u32[]{:S(2)}) %copy-start) | copy-done | bytes 1048600
  1.9 0.0 copy-start.1
  1.9 0.7 copy-done.1
  2.7 0.0 copy-start.2
  2.7 0.0 copy-start.3
  2.7 8.7 %prep.1 = (bf16[48,128]{1,0:T(8,128)(2,1)S(1)}, bf16[64,16,512]{2,1,0:T(8,128)(2,1)S(1)}, f32[16,128]{1,0:T(8,128)S(1)}) custom-call(bf16[512,1024]{1,0:T(8,128)(2,1)S(1)} %bitcast.6, s32[48,128]{1,0:T(8,128)S(1)} %bitcast.7, s32[1,256]{1,0:T(1,128)S(1)} %bitcast.11, s32[1,256]{1,0:T(1,128)S(1)} %bitcast.12), custom_call_target="tpu_custom_call" | custom-call | tf_op jit(solution)/shard_map/prep/pallas_call | solution.py:84
  11.3 0.0 copy-done.2
  11.3 0.0 copy-done.3
  11.3 86.9 %spread.1 = (f32[2,72,128]{2,1,0:T(8,128)S(1)}, bf16[64,16,512]{2,1,0:T(8,128)(2,1)S(1)}) custom-call(bf16[48,128]{1,0:T(8,128)(2,1)S(1)} %get-tuple-element.10.vals, s32[48,128]{1,0:T(8,128)S(1)} %bitcast.8, f32[48,128]{1,0:T(8,128)S(1)} %bitcast.9, f32[48,128]{1,0:T(8,128)S(1)} %bitcast.10, f32[16,128]{1,0:T(8,128)S(1)} %get-tuple-element.11.coords, ...), custom_call_target="tpu_custom_call" | custom-call | tf_op jit(solution)/shard_map/spread/pallas_call | solution.py:300
  98.2 9.4 %finish.1 = bf16[64,2,4,1024]{3,2,1,0:T(4,128)(2,1)} custom-call(f32[2,72,128]{2,1,0:T(8,128)S(1)} %get-tuple-element.13.gsum, f32[16,128]{1,0:T(8,128)S(1)} %get-tuple-element.11.coords, bf16[64,16,512]{2,1,0:T(8,128)(2,1)S(1)} %get-tuple-element.14.recv), custom_call_target="tpu_custom_call" | custom-call | tf_op jit(solution)/shard_map/finish/pallas_call | solution.py:396
Async XLA Ops:
  0.0 0.7 copy-start.5
  0.0 0.7 copy-start.4
  0.7 1.2 %copy-start = (bf16[1,2,256,1024]{3,2,1,0:T(8,128)(2,1)S(1)}, bf16[1,2,256,1024]{3,2,1,0:T(8,128)(2,1)}, u32[]{:S(2)}) copy-start(bf16[1,2,256,1024]{3,2,1,0:T(8,128)(2,1)} %param.6) | copy-start | bytes 3145732
  1.9 0.7 copy-start.1
  2.7 8.7 %copy-start.2 = (f32[1,6144]{1,0:T(1,128)S(1)}, f32[1,6144]{1,0:T(1,128)}, u32[]{:S(2)}) copy-start(f32[1,6144]{1,0:T(1,128)} %param.8) | copy-start | bytes 73732
  2.7 8.7 %copy-start.3 = (f32[1,6144]{1,0:T(1,128)S(1)}, f32[1,6144]{1,0:T(1,128)}, u32[]{:S(2)}) copy-start(f32[1,6144]{1,0:T(1,128)} %param.9) | copy-start | bytes 73732

commit v2 on v1

--- a/solution.py
+++ b/solution.py
@@ -10,7 +10,6 @@
 CAP = 4
 OWNERS = 64
 MEMBERS = 64
-STRIPS = 8
 TILES = 256
 CELLS = 1024
 STRIPW = 256
@@ -18,13 +17,12 @@
 FIRST_ROW = 112
 LENGTH_SQ = (STRIPW / 2.0) ** 2
 BLK = 72
+EARLY = 8
 MESH = pl.DeviceIdType.MESH
-VLIM = 48 * 1024 * 1024
-
-
-def prep_kernel(prior, idx, mask, holder, vals, outg, coords, fvals):
-    strip = lax.axis_index("tile")
-    mine = lax.axis_index("ens")
+VLIM = 56 * 1024 * 1024
+
+
+def pick_tiles(prior, mask, holder, outg, coords, strip, mine):
     owner = holder[...]
     wet = mask[...] == 1
     key = jnp.where(wet, owner, -1).astype(jnp.float32)
@@ -59,12 +57,14 @@
         total = part if total is None else total + part
     outg[...] = total.astype(jnp.bfloat16).reshape(OWNERS, 16, 512)
 
+
+def gather_rows(prior, idx, fvals, first, count):
     def step(j, carry):
-        ids = idx[pl.ds(j * 4, 4), :]
+        base = first + j * 4
         pieces, highs = [], []
         cell = lax.broadcasted_iota(jnp.int32, (CELLS, 128), 0)
         for i in range(4):
-            row = ids[i : i + 1, :]
+            row = idx[pl.ds(base + i, 1), :]
             pieces.append(jnp.where(cell == (row & (CELLS - 1)), 1.0, 0.0).astype(jnp.bfloat16))
             highs.append((row >> 10) - FIRST_ROW)
         onehot = jnp.concatenate(pieces, axis=1)
@@ -73,27 +73,10 @@
         line = lax.broadcasted_iota(jnp.int32, got.shape, 0)
         value = jnp.sum(jnp.where(line == high, got, 0.0), axis=0, keepdims=True)
         for i in range(4):
-            fvals[pl.ds(j * 4 + i, 1), :] = value[:, i * 128 : (i + 1) * 128]
-        return carry
-
-    lax.fori_loop(0, ROWS // 4, step, 0)
-    vals[...] = fvals[...].astype(jnp.bfloat16)
-
-
-def prep(prior, idx, mask, holder):
-    return pl.pallas_call(
-        prep_kernel,
-        out_shape=(
-            jax.ShapeDtypeStruct((ROWS, 128), jnp.bfloat16),
-            jax.ShapeDtypeStruct((OWNERS, 16, 512), jnp.bfloat16),
-            jax.ShapeDtypeStruct((16, 128), jnp.float32),
-        ),
-        in_specs=[pl.BlockSpec(memory_space=pltpu.VMEM)] * 4,
-        out_specs=[pl.BlockSpec(memory_space=pltpu.VMEM)] * 3,
-        scratch_shapes=[pltpu.VMEM((ROWS, 128), jnp.float32)],
-        compiler_params=pltpu.CompilerParams(vmem_limit_bytes=VLIM),
-        name="prep",
-    )(prior, idx, mask, holder)
+            fvals[pl.ds(base + i, 1), :] = value[:, i * 128 : (i + 1) * 128]
+        return carry
+
+    lax.fori_loop(0, count // 4, step, 0)
 
 
 def weights_into(wscr, idx, noise, tlat, tlon, strip):
@@ -117,25 +100,22 @@
 
 
 def gram_steps(fbuf, rows, first, wscr, read, acc):
+    count = 8
+
     def step(k, carry):
-        r0 = 2 * k
+        r0 = count * k
+        take = range(count)
         x = jnp.concatenate(
-            [fbuf[pl.ds(r0 + i, MEMBERS, stride=rows), :] for i in range(2)], axis=1
+            [fbuf[pl.ds(r0 + i, MEMBERS, stride=rows), :] for i in take], axis=1
         )
         mean = jnp.sum(x, axis=0, keepdims=True) * (1.0 / MEMBERS)
         dev = x - mean
-        reading = jnp.concatenate([read[pl.ds(first + r0 + i, 1), :] for i in range(2)], axis=1)
+        reading = jnp.concatenate([read[pl.ds(first + r0 + i, 1), :] for i in take], axis=1)
         inno = reading - mean
-        w = jnp.concatenate([wscr[first + r0], wscr[first + r0 + 1]], axis=1)
+        w = jnp.concatenate([wscr[first + r0 + i] for i in take], axis=1)
         high, low = split(dev)
         right = jnp.concatenate([high, low], axis=0)
-        winno = w * inno
-        top = lax.broadcasted_iota(jnp.int32, (8, 256), 0) == 0
-        blocks = []
-        for t in range(12):
-            blocks.append(dev * w[t : t + 1, :])
-            blocks.append(jnp.where(top, winno[t : t + 1, :], 0.0))
-        left = jnp.concatenate(blocks, axis=0)
+        left = jnp.concatenate([dev * w[t : t + 1, :] for t in range(12)] + [w * inno], axis=0)
         lh, ll = split(left)
         dims = (((1,), (1,)), ((), ()))
         acc[...] += lax.dot_general(
@@ -143,23 +123,36 @@
         ) + lax.dot_general(ll, right, dims, preferred_element_type=jnp.float32)
         return carry
 
-    lax.fori_loop(0, rows // 2, step, 0)
+    lax.fori_loop(0, rows // count, step, 0)
 
 
 def main_kernel(
-    vals, idx, read, noise, coords, outg, gsum, recv,
-    buf_a, buf_b, fa, fb, wscr, cbuf, acc, gp, gr, tot, lr,
+    prior_in, idx_in, mask_in, holder_in, read_in, noise_in, gsum, recv, coords,
+    prior, idx, mask, holder, read, noise, s_in, outg, vals, fvals, buf_a, buf_b, fa, fb, wscr, cown, cbuf, acc, gp, gr, tot, lr,
     s_own, s_a1, r_a1, s_b1, r_b1, s_a2, r_a2, s_b2, r_b2,
     s_x, r_x, s_c, r_c, s_g, r_g, s_l, r_l,
 ):
+    strips = lax.axis_size("tile")
     strip = lax.axis_index("tile")
     ens = lax.axis_index("ens")
     lev = lax.axis_index("lev")
     y, z = ens % 8, ens // 8
     i1, i2 = y + lev * (z - y), z + lev * (y - z)
     n1, n2 = 1 + 7 * lev, 8 - 7 * lev
-    low, high = (strip + STRIPS - 1) % STRIPS, (strip + 1) % STRIPS
-
+    low, high = (strip + strips - 1) % strips, (strip + 1) % strips
+    sign = 1 - 2 * lev
+
+    loads = [
+        pltpu.make_async_copy(src, dst, s_in.at[i])
+        for i, (src, dst) in enumerate(
+            (
+                (mask_in, mask), (holder_in, holder), (prior_in, prior),
+                (idx_in, idx), (read_in, read), (noise_in, noise),
+            )
+        )
+    ]
+    for load in loads:
+        load.start()
     barrier = pltpu.get_barrier_semaphore()
 
     def greet(d, carry):
@@ -171,6 +164,11 @@
     lax.fori_loop(1, OWNERS, greet, 0)
     for where in ({"tile": low}, {"tile": high}, {"lev": 1 - lev}):
         pl.semaphore_signal(barrier, inc=1, device_id=where, device_id_type=MESH)
+
+    for load in loads:
+        load.wait()
+    pick_tiles(prior, mask, holder, outg, cown, strip, ens)
+    coords[...] = cown[...]
     pl.semaphore_wait(barrier, OWNERS - 1 + 3)
 
     def send(src, dst, ss, rs, where):
@@ -182,14 +180,26 @@
     def wait_for(ref, sem):
         pltpu.make_async_copy(ref, ref, sem).wait()
 
+    def to(dy, dz):
+        other = (y + sign * dy + 16) % 8 + 8 * ((z + sign * dz + 16) % 8)
+        send(outg.at[other], recv.at[ens], s_x, r_x, {"ens": other})
+
+    def turn(k, carry):
+        u, v = 1 + k // 4, k % 4
+        to(u, v)
+        to(-v, u)
+        to(-u, -v)
+        to(v, -u)
+        return carry
+
+    own_x = pltpu.make_async_copy(outg.at[ens], recv.at[ens], s_own.at[2])
+    own_x.start()
+    send(cown, cbuf.at[1], s_c.at[0], r_c.at[1], {"tile": low})
+    send(cown, cbuf.at[0], s_c.at[1], r_c.at[0], {"tile": high})
+    lax.fori_loop(0, EARLY, turn, 0)
+
     own_a = pltpu.make_async_copy(vals.at[pl.ds(0, 32)], buf_a.at[i2, i1], s_own.at[0])
     own_b = pltpu.make_async_copy(vals.at[pl.ds(32, 16)], buf_b.at[i1, i2], s_own.at[1])
-    own_x = pltpu.make_async_copy(outg.at[ens], recv.at[ens], s_own.at[2])
-    own_a.start()
-    own_b.start()
-
-    send(coords, cbuf.at[1], s_c.at[0], r_c.at[1], {"tile": low})
-    send(coords, cbuf.at[0], s_c.at[1], r_c.at[0], {"tile": high})
 
     def first_a(d, carry):
         p = (i1 + d) % 8
@@ -211,31 +221,35 @@
         send(buf_b.at[i1], buf_b.at[i1], s_b2, r_b2, {"ens": p * n1 + i2 * n2})
         return carry
 
+    gather_rows(prior, idx, fvals, 32, 16)
+    vals[32:48] = fvals[32:48].astype(jnp.bfloat16)
+    own_b.start()
+    lax.fori_loop(1, 8, first_b, 0)
+    gather_rows(prior, idx, fvals, 0, 32)
+    vals[0:32] = fvals[0:32].astype(jnp.bfloat16)
+    own_a.start()
     lax.fori_loop(1, 8, first_a, 0)
-    lax.fori_loop(1, 8, first_b, 0)
+    own_b.wait()
+    wait_for(buf_b.at[0, pl.ds(0, 7)], r_b1)
+    lax.fori_loop(1, 8, second_b, 0)
+
+    wait_for(cbuf.at[0], r_c.at[0])
+    wait_for(cbuf.at[1], r_c.at[1])
+    pad = jnp.zeros((4, 128), jnp.float32)
+    tlat = jnp.concatenate([cbuf[0, 0:4], cown[0:4], cbuf[1, 0:4], pad], axis=0)
+    tlon = jnp.concatenate([cbuf[0, 4:8], cown[4:8], cbuf[1, 4:8], pad], axis=0)
+    weights_into(wscr, idx, noise, tlat, tlon, strip)
+    acc[...] = jnp.zeros_like(acc)
+
     own_a.wait()
     wait_for(buf_a.at[0, pl.ds(0, 7)], r_a1)
     lax.fori_loop(1, 8, second_a, 0)
-    own_b.wait()
-    wait_for(buf_b.at[0, pl.ds(0, 7)], r_b1)
-    lax.fori_loop(1, 8, second_b, 0)
-
-    own_x.start()
-
-    def exchange(d, carry):
-        other = (ens + d) % OWNERS
-        send(outg.at[other], recv.at[ens], s_x, r_x, {"ens": other})
-        return carry
-
-    lax.fori_loop(1, OWNERS, exchange, 0)
-
-    wait_for(cbuf.at[0], r_c.at[0])
-    wait_for(cbuf.at[1], r_c.at[1])
-    pad = jnp.zeros((4, 128), jnp.float32)
-    tlat = jnp.concatenate([cbuf[0, 0:4], coords[0:4], cbuf[1, 0:4], pad], axis=0)
-    tlon = jnp.concatenate([cbuf[0, 4:8], coords[4:8], cbuf[1, 4:8], pad], axis=0)
-    weights_into(wscr, idx, noise, tlat, tlon, strip)
-    acc[...] = jnp.zeros_like(acc)
+
+    lax.fori_loop(EARLY, 12, turn, 0)
+    lax.fori_loop(13, 16, turn, 0)
+    to(4, 4)
+    to(4, 0)
+    to(0, 4)
 
     wait_for(buf_b.at[pl.ds(0, 7)], r_b2)
 
@@ -259,14 +273,18 @@
     lax.fori_loop(0, MEMBERS, widen_a, 0)
     gram_steps(fa, 32, 0, wscr, read, acc)
 
+    pad = jnp.zeros((6, 128), jnp.float32)
     for g in range(3):
         for p in range(2):
-            sides = []
+            sides, tails = [], []
             for q in range(2):
                 t = g * 4 + p * 2 + q
-                block = acc[t * BLK : (t + 1) * BLK, :]
+                block = acc[t * MEMBERS : (t + 1) * MEMBERS, :]
                 sides.append(block[:, :64] + block[:, 64:])
-            gp[g, p] = jnp.concatenate(sides, axis=1)
+                line = acc[12 * MEMBERS + t : 12 * MEMBERS + t + 1, :]
+                tails.append(line[:, :64] + line[:, 64:])
+            gp[g, p, 0:64] = jnp.concatenate(sides, axis=1)
+            gp[g, p, 64:BLK] = jnp.broadcast_to(jnp.concatenate(tails, axis=1), (8, 128))
     send(gp.at[0], gr.at[1], s_g.at[0], r_g.at[1], {"tile": low})
     send(gp.at[2], gr.at[0], s_g.at[1], r_g.at[0], {"tile": high})
     wait_for(gr.at[0], r_g.at[0])
@@ -274,7 +292,7 @@
     tot[...] = (
         gp[1]
         + jnp.where(strip > 0, gr[0], jnp.zeros_like(gr[0]))
-        + jnp.where(strip < STRIPS - 1, gr[1], jnp.zeros_like(gr[1]))
+        + jnp.where(strip < strips - 1, gr[1], jnp.zeros_like(gr[1]))
     )
     send(tot, lr, s_l, r_l, {"lev": 1 - lev})
     wait_for(lr, r_l)
@@ -288,12 +306,12 @@
     wait_for(buf_a.at[pl.ds(0, 7)], s_a2)
     wait_for(buf_b.at[pl.ds(0, 7)], s_b2)
     for i in range(2):
-        wait_for(coords, s_c.at[i])
+        wait_for(cown, s_c.at[i])
         wait_for(gp.at[0], s_g.at[i])
     wait_for(tot, s_l)
 
 
-def spread_out(vals, idx, read, noise, coords, outg):
+def spread_out(prior, idx, mask, holder, read, noise):
     dma = pltpu.SemaphoreType.DMA
     vmem = pl.BlockSpec(memory_space=pltpu.VMEM)
     any_ = pl.BlockSpec(memory_space=pl.ANY)
@@ -302,17 +320,29 @@
         out_shape=(
             jax.ShapeDtypeStruct((2, BLK, 128), jnp.float32),
             jax.ShapeDtypeStruct((MEMBERS, 16, 512), jnp.bfloat16),
+            jax.ShapeDtypeStruct((16, 128), jnp.float32),
         ),
-        in_specs=[vmem] * 5 + [any_],
-        out_specs=[vmem, any_],
+        in_specs=[any_] * 6,
+        out_specs=[vmem, any_, vmem],
         scratch_shapes=[
+            pltpu.VMEM((2 * TILES, CELLS), jnp.bfloat16),
+            pltpu.VMEM((ROWS, 128), jnp.int32),
+            pltpu.VMEM((1, TILES), jnp.int32),
+            pltpu.VMEM((1, TILES), jnp.int32),
+            pltpu.VMEM((ROWS, 128), jnp.float32),
+            pltpu.VMEM((ROWS, 128), jnp.float32),
+            dma((6,)),
+            pltpu.VMEM((OWNERS, 16, 512), jnp.bfloat16),
+            pltpu.VMEM((ROWS, 128), jnp.bfloat16),
+            pltpu.VMEM((ROWS, 128), jnp.float32),
             pltpu.VMEM((8, 8, 32, 128), jnp.bfloat16),
             pltpu.VMEM((8, 8, 16, 128), jnp.bfloat16),
             pltpu.VMEM((MEMBERS * 32, 128), jnp.float32),
             pltpu.VMEM((MEMBERS * 16, 128), jnp.float32),
             pltpu.VMEM((ROWS, 16, 128), jnp.float32),
+            pltpu.VMEM((16, 128), jnp.float32),
             pltpu.VMEM((2, 16, 128), jnp.float32),
-            pltpu.VMEM((12 * BLK, 128), jnp.float32),
+            pltpu.VMEM((12 * MEMBERS + 16, 128), jnp.float32),
             pltpu.VMEM((3, 2, BLK, 128), jnp.float32),
             pltpu.VMEM((2, 2, BLK, 128), jnp.float32),
             pltpu.VMEM((2, BLK, 128), jnp.float32),
@@ -327,7 +357,7 @@
             collective_id=1, has_side_effects=True, vmem_limit_bytes=VLIM
         ),
         name="spread",
-    )(vals, idx, read, noise, coords, outg)
+    )(prior, idx, mask, holder, read, noise)
 
 
 def finish_kernel(gsum, coords, recv, out, wide, res):
@@ -347,20 +377,25 @@
         projs.append(pair[64:65])
     mats = [[m[8 * v : 8 * v + 8] for v in range(8)] for m in mats]
     sub = lax.broadcasted_iota(jnp.int32, (8, 128), 0)
-    for j in range(MEMBERS):
+    for j in range(0, MEMBERS, 2):
         v0, r = j // 8, j % 8
         for q in range(CAP):
             m = mats[q]
-            prow = m[v0][r : r + 1, :]
-            piv = prow[:, j : j + 1]
-            scaled = prow / piv
+            ra, rb = m[v0][r : r + 1, :], m[v0][r + 1 : r + 2, :]
+            pa = jnp.broadcast_to(ra[:, j : j + 1], (1, 128))
+            pb = jnp.broadcast_to(ra[:, j + 1 : j + 2], (1, 128))
+            pc = jnp.broadcast_to(rb[:, j + 1 : j + 2], (1, 128))
+            inv = 1.0 / pa
+            ratio = pb * inv
+            sa = ra * inv
+            sb = (rb - ratio * ra) / (pc - ratio * pb)
             for v in range(v0, 8):
-                col = m[v][:, j : j + 1]
+                ca = jnp.broadcast_to(m[v][:, j : j + 1], (8, 128))
+                cb = jnp.broadcast_to(m[v][:, j + 1 : j + 2], (8, 128)) - ca * ratio
                 if v == v0:
-                    if r == 7:
-                        continue
-                    col = jnp.where(sub[:, :1] > r, col, 0.0)
-                m[v] = m[v] - col * scaled
+                    ca = jnp.where(sub > r, ca, 0.0)
+                    cb = jnp.where(sub > r + 1, cb, 0.0)
+                m[v] = m[v] - ca * sa - cb * sb
     for q in range(CAP):
         m = jnp.concatenate(mats[q], axis=0)
         diag = jnp.sum(jnp.where(eye, m, 0.0), axis=1, keepdims=True)
@@ -412,8 +447,9 @@
     idx = location.reshape(ROWS, 128)
     read = reading.reshape(ROWS, 128)
     spread = noise.reshape(ROWS, 128)
-    vals, outg, coords = prep(prior, idx, ocean.reshape(1, TILES), holder.reshape(1, TILES))
-    gsum, recv = spread_out(vals, idx, read, spread, coords, outg)
+    gsum, recv, coords = spread_out(
+        prior, idx, ocean.reshape(1, TILES), holder.reshape(1, TILES), read, spread
+    )
     return finish(gsum, coords, recv)
 
 

time: 108 us -> 74.6 us (0.69)
  Pallas kernels: 105 us -> 74.4 us
  local copies, waits for them, and re-layouts: 2.66 us -> 0 us
    pallas_call x1, Pallas kernels: 86.9 us -> 65.1 us  [spread_out(): pl.pallas_call(main_kernel, out_shape=(jax.ShapeDtypeStruct((2, BLK, 128)...]
    pallas_call x1 -> x0, Pallas kernels: 8.65 us -> none  [prep(): pl.pallas_call(prep_kernel, out_shape=(jax.ShapeDtypeStruct((ROWS, 128),...]
    unnamed x12 -> x0, local copies, waits for them, and re-layouts: 2.66 us -> none
where the time goes in v2:
time: 74.6 us; the launch traced here: 74.4 us
  Pallas kernels  74.4 us (100%)
    pallas_call x1, Pallas kernels, spread_out(): pl.pallas_call(main_kernel, out_shape=(jax.ShapeDtypeStruct((2, BLK, 128)...  65.1 us
    pallas_call x1, Pallas kernels, finish(): pl.pallas_call(finish_kernel, out_shape=jax.ShapeDtypeStruct((MEMBERS, 2,...  9.27 us

profile of v2, /device:TPU:1, one launch (start us, length us, event | category | flops | bytes accessed | tf_op | source)
XLA Modules:
  0.0 74.4 jit_solution(13450323443614695650)
XLA Ops:
  0.0 65.1 %spread.1 = (f32[2,72,128]{2,1,0:T(8,128)}, bf16[64,16,512]{2,1,0:T(8,128)(2,1)}, f32[16,128]{1,0:T(8,128)}) custom-call(bf16[512,1024]{1,0:T(8,128)(2,1)} %bitcast.6, s32[48,128]{1,0:T(8,128)} %bitcast.7, s32[1,256]{1,0:T(1,128)} %bitcast.10, s32[1,256]{1,0:T(1,128)} %bitcast.11, f32[48,128]{1,0:T(8,128)} %bitcast.8, f32[48,128]{1,0:T(8,128)} %bitcast.9), custom_call_target="tpu_custom_call" | custom-call | tf_op jit(solution)/shard_map/spread/pallas_call | solution.py:318
  65.1 9.3 %finish.1 = bf16[64,2,4,1024]{3,2,1,0:T(4,128)(2,1)} custom-call(f32[2,72,128]{2,1,0:T(8,128)} %get-tuple-element.8.gsum, f32[16,128]{1,0:T(8,128)} %get-tuple-element.9.coords, bf16[64,16,512]{2,1,0:T(8,128)(2,1)} %get-tuple-element.10.recv), custom_call_target="tpu_custom_call" | custom-call | tf_op jit(solution)/shard_map/finish/pallas_call | solution.py:431

commit v3 on v2

--- a/solution.py
+++ b/solution.py
@@ -58,25 +58,36 @@
     outg[...] = total.astype(jnp.bfloat16).reshape(OWNERS, 16, 512)
 
 
-def gather_rows(prior, idx, fvals, first, count):
+def one_hot(row):
+    line = lax.broadcasted_iota(jnp.int32, (32, 128), 0)
+    low = jnp.where(line == (row & 31), 1.0, 0.0).astype(jnp.bfloat16)
+    high = jnp.broadcast_to((row >> 5) & 31, (16, 128))
+    parts = []
+    for a in range(32):
+        here = jnp.where(high == a, 1.0, 0.0).astype(jnp.bfloat16)
+        parts.append(low * jnp.concatenate([here, here], axis=0))
+    return jnp.concatenate(parts, axis=0)
+
+
+def gather_rows(prior, idx, fvals, first, count, beside):
     def step(j, carry):
-        base = first + j * 4
+        beside(j)
+        base = first + j * 8
         pieces, highs = [], []
-        cell = lax.broadcasted_iota(jnp.int32, (CELLS, 128), 0)
-        for i in range(4):
+        for i in range(8):
             row = idx[pl.ds(base + i, 1), :]
-            pieces.append(jnp.where(cell == (row & (CELLS - 1)), 1.0, 0.0).astype(jnp.bfloat16))
+            pieces.append(one_hot(row))
             highs.append((row >> 10) - FIRST_ROW)
         onehot = jnp.concatenate(pieces, axis=1)
         high = jnp.concatenate(highs, axis=1)
         got = jnp.dot(prior[FIRST_ROW:, :], onehot, preferred_element_type=jnp.float32)
         line = lax.broadcasted_iota(jnp.int32, got.shape, 0)
         value = jnp.sum(jnp.where(line == high, got, 0.0), axis=0, keepdims=True)
-        for i in range(4):
+        for i in range(8):
             fvals[pl.ds(base + i, 1), :] = value[:, i * 128 : (i + 1) * 128]
         return carry
 
-    lax.fori_loop(0, count // 4, step, 0)
+    lax.fori_loop(0, count // 8, step, 0)
 
 
 def weights_into(wscr, idx, noise, tlat, tlon, strip):
@@ -99,11 +110,13 @@
     return high, low
 
 
-def gram_steps(fbuf, rows, first, wscr, read, acc):
+def gram_steps(fbuf, rows, first, wscr, read, acc, t0, count_t, beside=None):
     count = 8
 
     def step(k, carry):
         r0 = count * k
+        if beside is not None:
+            beside(k)
         take = range(count)
         x = jnp.concatenate(
             [fbuf[pl.ds(r0 + i, MEMBERS, stride=rows), :] for i in take], axis=1
@@ -115,7 +128,9 @@
         w = jnp.concatenate([wscr[first + r0 + i] for i in take], axis=1)
         high, low = split(dev)
         right = jnp.concatenate([high, low], axis=0)
-        left = jnp.concatenate([dev * w[t : t + 1, :] for t in range(12)] + [w * inno], axis=0)
+        left = jnp.concatenate(
+            [dev * w[t : t + 1, :] for t in range(t0, t0 + count_t)] + [w * inno], axis=0
+        )
         lh, ll = split(left)
         dims = (((1,), (1,)), ((), ()))
         acc[...] += lax.dot_general(
@@ -123,13 +138,68 @@
         ) + lax.dot_general(ll, right, dims, preferred_element_type=jnp.float32)
         return carry
 
-    lax.fori_loop(0, rows // count, step, 0)
+    lax.fori_loop(0, rows // count, step, 0, unroll=2)
+
+
+def transforms(gsum, coords, mats, out):
+    row = lax.broadcasted_iota(jnp.int32, (MEMBERS, 128), 0)
+    lane = lax.broadcasted_iota(jnp.int32, (MEMBERS, 128), 1)
+    sub = lax.broadcasted_iota(jnp.int32, (8, 128), 0)
+    for q in range(CAP):
+        pair = gsum[q // 2, 0:64]
+        if q % 2:
+            pair = jnp.concatenate([pair[:, 64:], pair[:, :64]], axis=1)
+        body = pair + jnp.where(row == lane, MEMBERS - 1.0, 0.0)
+        mats[q] = jnp.where(lane < 64, body, jnp.where(row + MEMBERS == lane, 1.0, 0.0))
+
+    def block(b, carry):
+        start = pl.multiple_of(b * 8, 8)
+        heads = [mats[q, pl.ds(start, 8), :] for q in range(CAP)]
+        parts = [[mats[q, 8 * v : 8 * v + 8, :] for v in range(8)] for q in range(CAP)]
+        for r in range(0, 8, 2):
+            for q in range(CAP):
+                ra, rb = heads[q][r : r + 1, :], heads[q][r + 1 : r + 2, :]
+                pa = jnp.broadcast_to(ra[:, r : r + 1], (1, 128))
+                pb = jnp.broadcast_to(ra[:, r + 1 : r + 2], (1, 128))
+                pc = jnp.broadcast_to(rb[:, r + 1 : r + 2], (1, 128))
+                inv = 1.0 / pa
+                ratio = pb * inv
+                sa = ra * inv
+                sb = (rb - ratio * ra) / (pc - ratio * pb)
+
+                def reduced(x, rows, pivot):
+                    ca = jnp.broadcast_to(x[:, r : r + 1], (8, 128))
+                    cb = jnp.broadcast_to(x[:, r + 1 : r + 2], (8, 128)) - ca * ratio
+                    ca = jnp.where(rows > pivot, ca, 0.0)
+                    cb = jnp.where(rows > pivot + 1, cb, 0.0)
+                    return x - ca * sa - cb * sb
+
+                heads[q] = reduced(heads[q], sub, r)
+                for v in range(8):
+                    parts[q][v] = reduced(parts[q][v], sub + 8 * v, start + r)
+        for q in range(CAP):
+            for v in range(8):
+                mats[q, 8 * v : 8 * v + 8, :] = pltpu.roll(parts[q][v], 120, 1)
+        return carry
+
+    lax.fori_loop(0, 8, block, 0)
+    for q in range(CAP):
+        m = mats[q]
+        diag = jnp.sum(jnp.where(row + MEMBERS == lane, m, 0.0), axis=1, keepdims=True)
+        inv = m[:, :64] * lax.rsqrt(diag)
+        proj = gsum[q // 2, 64:65]
+        proj = proj[:, 64:] if q % 2 else proj[:, :64]
+        zed = jnp.sum(inv * proj, axis=1, keepdims=True)
+        mean_w = jnp.sum(inv * zed, axis=0, keepdims=True)
+        trans = inv * (MEMBERS - 1.0) ** 0.5 + mean_w
+        trans = trans + (1.0 - jnp.sum(trans, axis=1, keepdims=True)) * (1.0 / MEMBERS)
+        out[q] = trans * coords[8 + q : 9 + q, :64]
 
 
 def main_kernel(
-    prior_in, idx_in, mask_in, holder_in, read_in, noise_in, gsum, recv, coords,
-    prior, idx, mask, holder, read, noise, s_in, outg, vals, fvals, buf_a, buf_b, fa, fb, wscr, cown, cbuf, acc, gp, gr, tot, lr,
-    s_own, s_a1, r_a1, s_b1, r_b1, s_a2, r_a2, s_b2, r_b2,
+    prior_in, idx_in, mask_in, holder_in, read_in, noise_in, trans, recv,
+    prior, idx, mask, holder, read, noise, s_in, outg, vals, fvals, buf_a, buf_b, fa, fb, wscr, cown, cbuf, acc, acc_own, gp, gr, tot, lr,
+    tot2, mats, s_own, s_a1, r_a1, s_b1, r_b1, s_a2, r_a2, s_b2, r_b2,
     s_x, r_x, s_c, r_c, s_g, r_g, s_l, r_l,
 ):
     strips = lax.axis_size("tile")
@@ -168,7 +238,6 @@
     for load in loads:
         load.wait()
     pick_tiles(prior, mask, holder, outg, cown, strip, ens)
-    coords[...] = cown[...]
     pl.semaphore_wait(barrier, OWNERS - 1 + 3)
 
     def send(src, dst, ss, rs, where):
@@ -196,7 +265,6 @@
     own_x.start()
     send(cown, cbuf.at[1], s_c.at[0], r_c.at[1], {"tile": low})
     send(cown, cbuf.at[0], s_c.at[1], r_c.at[0], {"tile": high})
-    lax.fori_loop(0, EARLY, turn, 0)
 
     own_a = pltpu.make_async_copy(vals.at[pl.ds(0, 32)], buf_a.at[i2, i1], s_own.at[0])
     own_b = pltpu.make_async_copy(vals.at[pl.ds(32, 16)], buf_b.at[i1, i2], s_own.at[1])
@@ -211,45 +279,40 @@
         send(vals.at[pl.ds(32, 16)], buf_b.at[i1, i2], s_b1, r_b1, {"ens": i1 * n1 + p * n2})
         return carry
 
-    def second_a(d, carry):
-        p = (i2 + d) % 8
-        send(buf_a.at[i2], buf_a.at[i2], s_a2, r_a2, {"ens": i1 * n1 + p * n2})
-        return carry
-
-    def second_b(d, carry):
-        p = (i1 + d) % 8
-        send(buf_b.at[i1], buf_b.at[i1], s_b2, r_b2, {"ens": p * n1 + i2 * n2})
-        return carry
-
-    gather_rows(prior, idx, fvals, 32, 16)
+    def along(i, j, ni, nj):
+        return {"ens": i * ni + j * nj}
+
+    def second(buf, i, j, ni, nj, ss, rs):
+        for d in (4, 3, 5, 2, 6, 1, 7):
+            send(buf.at[j], buf.at[j], ss, rs, along(i, (j + d) % 8, ni, nj))
+
+    side_a = (buf_a, i1, i2, n1, n2)
+    side_b = (buf_b, i2, i1, n2, n1)
+
+    gather_rows(prior, idx, fvals, 32, 16, lambda j: (turn(2 * j, 0), turn(2 * j + 1, 0)))
     vals[32:48] = fvals[32:48].astype(jnp.bfloat16)
     own_b.start()
     lax.fori_loop(1, 8, first_b, 0)
-    gather_rows(prior, idx, fvals, 0, 32)
+    gather_rows(prior, idx, fvals, 0, 32, lambda j: turn(4 + j, 0))
     vals[0:32] = fvals[0:32].astype(jnp.bfloat16)
     own_a.start()
     lax.fori_loop(1, 8, first_a, 0)
     own_b.wait()
     wait_for(buf_b.at[0, pl.ds(0, 7)], r_b1)
-    lax.fori_loop(1, 8, second_b, 0)
+    second(*side_b, s_b2, r_b2)
 
     wait_for(cbuf.at[0], r_c.at[0])
     wait_for(cbuf.at[1], r_c.at[1])
     pad = jnp.zeros((4, 128), jnp.float32)
-    tlat = jnp.concatenate([cbuf[0, 0:4], cown[0:4], cbuf[1, 0:4], pad], axis=0)
-    tlon = jnp.concatenate([cbuf[0, 4:8], cown[4:8], cbuf[1, 4:8], pad], axis=0)
+    tlat = jnp.concatenate([cbuf[0, 0:4], cbuf[1, 0:4], cown[0:4], pad], axis=0)
+    tlon = jnp.concatenate([cbuf[0, 4:8], cbuf[1, 4:8], cown[4:8], pad], axis=0)
     weights_into(wscr, idx, noise, tlat, tlon, strip)
     acc[...] = jnp.zeros_like(acc)
+    acc_own[...] = jnp.zeros_like(acc_own)
 
     own_a.wait()
     wait_for(buf_a.at[0, pl.ds(0, 7)], r_a1)
-    lax.fori_loop(1, 8, second_a, 0)
-
-    lax.fori_loop(EARLY, 12, turn, 0)
-    lax.fori_loop(13, 16, turn, 0)
-    to(4, 4)
-    to(4, 0)
-    to(0, 4)
+    second(*side_a, s_a2, r_a2)
 
     wait_for(buf_b.at[pl.ds(0, 7)], r_b2)
 
@@ -260,7 +323,19 @@
         return carry
 
     lax.fori_loop(0, MEMBERS, widen_b, 0)
-    gram_steps(fb, 16, 32, wscr, read, acc)
+
+    def some(k):
+        turn(8 + 2 * k, 0)
+        turn(9 + 2 * k, 0)
+        turn(13 + k, 0)
+
+    gram_steps(fb, 16, 32, wscr, read, acc, 0, 8, some)
+    turn(15, 0)
+    to(4, 4)
+    to(4, 0)
+    to(0, 4)
+
+    gram_steps(fb, 16, 32, wscr, read, acc_own, 8, 4)
 
     wait_for(buf_a.at[pl.ds(0, 7)], r_a2)
 
@@ -271,32 +346,38 @@
         return carry
 
     lax.fori_loop(0, MEMBERS, widen_a, 0)
-    gram_steps(fa, 32, 0, wscr, read, acc)
-
-    pad = jnp.zeros((6, 128), jnp.float32)
-    for g in range(3):
+    gram_steps(fa, 32, 0, wscr, read, acc, 0, 8)
+
+    def pack(src, rows, first, count, dst):
         for p in range(2):
             sides, tails = [], []
             for q in range(2):
-                t = g * 4 + p * 2 + q
-                block = acc[t * MEMBERS : (t + 1) * MEMBERS, :]
+                t = first + p * 2 + q
+                block = src[t * MEMBERS : (t + 1) * MEMBERS, :]
                 sides.append(block[:, :64] + block[:, 64:])
-                line = acc[12 * MEMBERS + t : 12 * MEMBERS + t + 1, :]
+                at = count * MEMBERS + rows + p * 2 + q
+                line = src[at : at + 1, :]
                 tails.append(line[:, :64] + line[:, 64:])
-            gp[g, p, 0:64] = jnp.concatenate(sides, axis=1)
-            gp[g, p, 64:BLK] = jnp.broadcast_to(jnp.concatenate(tails, axis=1), (8, 128))
+            dst[p, 0:64] = jnp.concatenate(sides, axis=1)
+            dst[p, 64:BLK] = jnp.broadcast_to(jnp.concatenate(tails, axis=1), (8, 128))
+
+    pack(acc, 0, 0, 8, gp.at[0])
     send(gp.at[0], gr.at[1], s_g.at[0], r_g.at[1], {"tile": low})
-    send(gp.at[2], gr.at[0], s_g.at[1], r_g.at[0], {"tile": high})
+    pack(acc, 4, 4, 8, gp.at[1])
+    send(gp.at[1], gr.at[0], s_g.at[1], r_g.at[0], {"tile": high})
+    gram_steps(fa, 32, 0, wscr, read, acc_own, 8, 4)
+    pack(acc_own, 8, 0, 4, gp.at[2])
     wait_for(gr.at[0], r_g.at[0])
     wait_for(gr.at[1], r_g.at[1])
     tot[...] = (
-        gp[1]
+        gp[2]
         + jnp.where(strip > 0, gr[0], jnp.zeros_like(gr[0]))
         + jnp.where(strip < strips - 1, gr[1], jnp.zeros_like(gr[1]))
     )
     send(tot, lr, s_l, r_l, {"lev": 1 - lev})
     wait_for(lr, r_l)
-    gsum[...] = tot[...] + lr[...]
+    tot2[...] = tot[...] + lr[...]
+    transforms(tot2, cown, mats, trans)
 
     own_x.wait()
     wait_for(recv.at[pl.ds(0, OWNERS - 1)], r_x)
@@ -318,12 +399,11 @@
     return pl.pallas_call(
         main_kernel,
         out_shape=(
-            jax.ShapeDtypeStruct((2, BLK, 128), jnp.float32),
+            jax.ShapeDtypeStruct((CAP, MEMBERS, MEMBERS), jnp.float32),
             jax.ShapeDtypeStruct((MEMBERS, 16, 512), jnp.bfloat16),
-            jax.ShapeDtypeStruct((16, 128), jnp.float32),
         ),
         in_specs=[any_] * 6,
-        out_specs=[vmem, any_, vmem],
+        out_specs=[vmem, any_],
         scratch_shapes=[
             pltpu.VMEM((2 * TILES, CELLS), jnp.bfloat16),
             pltpu.VMEM((ROWS, 128), jnp.int32),
@@ -342,11 +422,14 @@
             pltpu.VMEM((ROWS, 16, 128), jnp.float32),
             pltpu.VMEM((16, 128), jnp.float32),
             pltpu.VMEM((2, 16, 128), jnp.float32),
-            pltpu.VMEM((12 * MEMBERS + 16, 128), jnp.float32),
+            pltpu.VMEM((8 * MEMBERS + 16, 128), jnp.float32),
+            pltpu.VMEM((4 * MEMBERS + 16, 128), jnp.float32),
             pltpu.VMEM((3, 2, BLK, 128), jnp.float32),
             pltpu.VMEM((2, 2, BLK, 128), jnp.float32),
             pltpu.VMEM((2, BLK, 128), jnp.float32),
             pltpu.VMEM((2, BLK, 128), jnp.float32),
+            pltpu.VMEM((2, BLK, 128), jnp.float32),
+            pltpu.VMEM((CAP, MEMBERS, 128), jnp.float32),
             dma((3,)),
             dma, dma, dma, dma, dma, dma, dma, dma,
             dma, dma,
@@ -360,54 +443,12 @@
     )(prior, idx, mask, holder, read, noise)
 
 
-def finish_kernel(gsum, coords, recv, out, wide, res):
+def finish_kernel(trans, recv, out, wide, res):
     for c in range(4):
         wide[c] = recv[:, :, c * 128 : (c + 1) * 128].astype(jnp.float32).reshape(-1, 128)
-    row = lax.broadcasted_iota(jnp.int32, (MEMBERS, 128), 0)
-    lane = lax.broadcasted_iota(jnp.int32, (MEMBERS, 128), 1)
-    eye = row == lane
-    eye_r = row + MEMBERS == lane
-    mats, projs = [], []
     for q in range(CAP):
-        pair = gsum[q // 2]
-        if q % 2:
-            pair = jnp.concatenate([pair[:, 64:], pair[:, :64]], axis=1)
-        body = pair[:64] + jnp.where(eye, MEMBERS - 1.0, 0.0)
-        mats.append(jnp.where(lane < 64, body, jnp.where(eye_r, 1.0, 0.0)))
-        projs.append(pair[64:65])
-    mats = [[m[8 * v : 8 * v + 8] for v in range(8)] for m in mats]
-    sub = lax.broadcasted_iota(jnp.int32, (8, 128), 0)
-    for j in range(0, MEMBERS, 2):
-        v0, r = j // 8, j % 8
-        for q in range(CAP):
-            m = mats[q]
-            ra, rb = m[v0][r : r + 1, :], m[v0][r + 1 : r + 2, :]
-            pa = jnp.broadcast_to(ra[:, j : j + 1], (1, 128))
-            pb = jnp.broadcast_to(ra[:, j + 1 : j + 2], (1, 128))
-            pc = jnp.broadcast_to(rb[:, j + 1 : j + 2], (1, 128))
-            inv = 1.0 / pa
-            ratio = pb * inv
-            sa = ra * inv
-            sb = (rb - ratio * ra) / (pc - ratio * pb)
-            for v in range(v0, 8):
-                ca = jnp.broadcast_to(m[v][:, j : j + 1], (8, 128))
-                cb = jnp.broadcast_to(m[v][:, j + 1 : j + 2], (8, 128)) - ca * ratio
-                if v == v0:
-                    ca = jnp.where(sub > r, ca, 0.0)
-                    cb = jnp.where(sub > r + 1, cb, 0.0)
-                m[v] = m[v] - ca * sa - cb * sb
-    for q in range(CAP):
-        m = jnp.concatenate(mats[q], axis=0)
-        diag = jnp.sum(jnp.where(eye, m, 0.0), axis=1, keepdims=True)
-        inv = m[:, 64:] * lax.rsqrt(diag)
-        proj = projs[q][:, :64]
-        zed = jnp.sum(inv * proj, axis=1, keepdims=True)
-        mean_w = jnp.sum(inv * zed, axis=0, keepdims=True)
-        trans = inv * (MEMBERS - 1.0) ** 0.5 + mean_w
-        trans = trans + (1.0 - jnp.sum(trans, axis=1, keepdims=True)) * (1.0 / MEMBERS)
-        trans = trans * coords[8 + q : 9 + q, :64]
-        t0 = trans.astype(jnp.bfloat16)
-        rest = trans - t0.astype(jnp.float32)
+        t0 = trans[q].astype(jnp.bfloat16)
+        rest = trans[q] - t0.astype(jnp.float32)
         t1, t2 = split(rest)
         left = jnp.concatenate([t0, t1, t2], axis=0)
         for v in range(2):
@@ -427,11 +468,11 @@
         out[:, :, :, c * 128 : (c + 1) * 128] = body
 
 
-def finish(gsum, coords, recv):
+def finish(trans, recv):
     return pl.pallas_call(
         finish_kernel,
         out_shape=jax.ShapeDtypeStruct((MEMBERS, 2, CAP, CELLS), jnp.bfloat16),
-        in_specs=[pl.BlockSpec(memory_space=pltpu.VMEM)] * 3,
+        in_specs=[pl.BlockSpec(memory_space=pltpu.VMEM)] * 2,
         out_specs=pl.BlockSpec(memory_space=pltpu.VMEM),
         scratch_shapes=[
             pltpu.VMEM((4, MEMBERS * 16, 128), jnp.float32),
@@ -439,7 +480,7 @@
         ],
         compiler_params=pltpu.CompilerParams(vmem_limit_bytes=VLIM),
         name="finish",
-    )(gsum, coords, recv)
+    )(trans, recv)
 
 
 def local(prior, location, reading, noise, ocean, holder):
@@ -447,10 +488,10 @@
     idx = location.reshape(ROWS, 128)
     read = reading.reshape(ROWS, 128)
     spread = noise.reshape(ROWS, 128)
-    gsum, recv, coords = spread_out(
+    trans, recv = spread_out(
         prior, idx, ocean.reshape(1, TILES), holder.reshape(1, TILES), read, spread
     )
-    return finish(gsum, coords, recv)
+    return finish(trans, recv)
 
 
 def solution(mesh):

time: 74.6 us -> 74.1 us (level)
  the two profiles are of different devices: /device:TPU:1 before, /device:TPU:165 now
where the time goes in v3:
time: 74.1 us; the launch traced here: 73.9 us
  Pallas kernels  73.9 us (100%)
    pallas_call x1, Pallas kernels, spread_out(): pl.pallas_call(main_kernel, out_shape=(jax.ShapeDtypeStruct((CAP, MEMBERS...  69.7 us
    pallas_call x1, Pallas kernels, finish(): pl.pallas_call(finish_kernel, out_shape=jax.ShapeDtypeStruct((MEMBERS, 2,...  4.2 us

profile of v3, /device:TPU:165, one launch (start us, length us, event | category | flops | bytes accessed | tf_op | source)
XLA Modules:
  0.0 73.9 jit_solution(13339634121896471991)
XLA Ops:
  0.0 69.7 %spread.1 = (f32[4,64,64]{2,1,0:T(8,128)}, bf16[64,16,512]{2,1,0:T(8,128)(2,1)}) custom-call(bf16[512,1024]{1,0:T(8,128)(2,1)} %bitcast.6, s32[48,128]{1,0:T(8,128)} %bitcast.7, s32[1,256]{1,0:T(1,128)} %bitcast.10, s32[1,256]{1,0:T(1,128)} %bitcast.11, f32[48,128]{1,0:T(8,128)} %bitcast.8, f32[48,128]{1,0:T(8,128)} %bitcast.9), custom_call_target="tpu_custom_call" | custom-call | tf_op jit(solution)/shard_map/spread/pallas_call | solution.py:399
  69.7 4.2 %finish.1 = bf16[64,2,4,1024]{3,2,1,0:T(4,128)(2,1)} custom-call(f32[4,64,64]{2,1,0:T(8,128)} %get-tuple-element.7.trans, bf16[64,16,512]{2,1,0:T(8,128)(2,1)} %get-tuple-element.8.recv), custom_call_target="tpu_custom_call" | custom-call | tf_op jit(solution)/shard_map/finish/pallas_call | solution.py:472

commit v4 on v3

--- a/solution.py
+++ b/solution.py
@@ -101,7 +101,7 @@
         wscr[r] = jnp.exp(-dist / (2.0 * LENGTH_SQ)) * (1.0 / noise[pl.ds(r, 1), :])
         return carry
 
-    lax.fori_loop(0, ROWS, step, 0)
+    lax.fori_loop(0, ROWS, step, 0, unroll=4)
 
 
 def split(x):
@@ -322,7 +322,7 @@
         fb[pl.ds(pl.multiple_of(m * 16, 16), 16), :] = buf_b[a, b].astype(jnp.float32)
         return carry
 
-    lax.fori_loop(0, MEMBERS, widen_b, 0)
+    lax.fori_loop(0, MEMBERS, widen_b, 0, unroll=8)
 
     def some(k):
         turn(8 + 2 * k, 0)
@@ -345,7 +345,7 @@
         fa[pl.ds(pl.multiple_of(m * 32, 32), 32), :] = buf_a[a, b].astype(jnp.float32)
         return carry
 
-    lax.fori_loop(0, MEMBERS, widen_a, 0)
+    lax.fori_loop(0, MEMBERS, widen_a, 0, unroll=8)
     gram_steps(fa, 32, 0, wscr, read, acc, 0, 8)
 
     def pack(src, rows, first, count, dst):

time: 74.1 us -> 74.1 us (level)
  no operation moved by 1% of the time
where the time goes in v4:
time: 74.1 us; the launch traced here: 73.9 us
  Pallas kernels  73.9 us (100%)
    pallas_call x1, Pallas kernels, spread_out(): pl.pallas_call(main_kernel, out_shape=(jax.ShapeDtypeStruct((CAP, MEMBERS...  69.7 us
    pallas_call x1, Pallas kernels, finish(): pl.pallas_call(finish_kernel, out_shape=jax.ShapeDtypeStruct((MEMBERS, 2,...  4.2 us

profile of v4, /device:TPU:165, one launch (start us, length us, event | category | flops | bytes accessed | tf_op | source)
XLA Modules:
  0.0 73.9 jit_solution(16832201462420542516)
XLA Ops:
  0.0 69.7 %spread.1 = (f32[4,64,64]{2,1,0:T(8,128)}, bf16[64,16,512]{2,1,0:T(8,128)(2,1)}) custom-call(bf16[512,1024]{1,0:T(8,128)(2,1)} %bitcast.6, s32[48,128]{1,0:T(8,128)} %bitcast.7, s32[1,256]{1,0:T(1,128)} %bitcast.10, s32[1,256]{1,0:T(1,128)} %bitcast.11, f32[48,128]{1,0:T(8,128)} %bitcast.8, f32[48,128]{1,0:T(8,128)} %bitcast.9), custom_call_target="tpu_custom_call" | custom-call | tf_op jit(solution)/shard_map/spread/pallas_call | solution.py:399
  69.7 4.2 %finish.1 = bf16[64,2,4,1024]{3,2,1,0:T(4,128)(2,1)} custom-call(f32[4,64,64]{2,1,0:T(8,128)} %get-tuple-element.7.trans, bf16[64,16,512]{2,1,0:T(8,128)(2,1)} %get-tuple-element.8.recv), custom_call_target="tpu_custom_call" | custom-call | tf_op jit(solution)/shard_map/finish/pallas_call | solution.py:472
